TPU v7x, 128 devices: a whole 4x4x4 slice. The times are simulated.
128 devices in a mesh: pipe: 4 (over x_hi, core), expert: 32 (over x_lo, y, z).
Axes of the slice: x: 4 (x_hi: 2, x_lo: 2; x = x_hi * 2 + x_lo), y: 4, z: 4, core: 2. Of those that a mesh axis runs over, the one named last changes fastest.
Arguments:
- held_a: bfloat16 [4, 1024, 7168], P('pipe', 'expert'), may hold values from -6 to 6
- held_b: bfloat16 [4, 1024, 7168], P('pipe', 'expert'), may hold values from -6 to 6
- new_a: bfloat16 [1024, 7168], P('expert'), may hold values from -6 to 6
- new_b: bfloat16 [1024, 7168], P('expert'), may hold values from -6 to 6
- expert_ids: int32 [4, 4, 1024, 2], P('pipe', None, 'expert'), may hold values from 0 to 7, all different within a row; in each aligned block of 32 rows (0 to 31, 32 to 63, ..., all dimensions but the last counted through in order) at most 10 rows name the same one
- route_probs: float32 [4, 4, 1024, 2], P('pipe', None, 'expert'), may hold values from 0.1 to 1
- saved_gate_up: bfloat16 [4, 4, 320, 2, 8192], P('pipe', None, None, None, 'expert'), may hold values from -8 to 8
- w_gate: bfloat16 [4, 7168, 8192], P('pipe', None, 'expert'), may hold values from -0.0625 to 0.0625
- w_up: bfloat16 [4, 7168, 8192], P('pipe', None, 'expert'), may hold values from -0.0625 to 0.0625
- w_down: bfloat16 [4, 8192, 7168], P('pipe', 'expert'), may hold values from -0.1875 to 0.1875
Outputs:
- first_a: bfloat16 [4, 1024, 7168], P('pipe', 'expert')
- first_b: bfloat16 [4, 1024, 7168], P('pipe', 'expert')
- second_a: bfloat16 [4, 1024, 7168], P('pipe', 'expert')
- second_b: bfloat16 [4, 1024, 7168], P('pipe', 'expert')
Inputs may be any that keep to these rules, and one draw needn't show every extreme that they name: `expert_ids`: in each aligned block of 32 tokens (one index of expert's tokens of one section and micro-batch) no expert is named by more than 10 tokens, a bound that some block reaches; each token names 2 different experts.
All inputs are finite; a program needn't handle non-finite values.
Results may differ from a plain program's by a relative error of at most 0.017.
Values may be sent and summed in bfloat16 or wider, within the bound.
A program may use at most 192 MiB of HBM per device.

v0:
```python
import jax
import jax.numpy as jnp
from jax import lax
from jax.sharding import PartitionSpec as P

EXPERTS = 8
TOPK = 2
CAP = 10


def passed_along(block, axis, distance):
    devices = range(lax.axis_size(axis))
    route = [(i - distance, i) for i in devices if i - distance in devices]
    return lax.ppermute(block, axis, route)


def route_layout(grads, route_ids, probs, slices):
    tok_rows = grads.shape[0]
    width = grads.shape[1]
    flat_ids = route_ids.reshape(-1)
    onehot = (flat_ids[:, None] == jnp.arange(EXPERTS, dtype=jnp.int32)[None, :]).astype(jnp.int32)
    ranking = jnp.sum((jnp.cumsum(onehot, axis=0) - 1) * onehot, axis=1)
    slot_ids = flat_ids * CAP + ranking
    dispatch = (slot_ids[None, :] == jnp.arange(EXPERTS * CAP, dtype=jnp.int32)[:, None]).astype(
        jnp.bfloat16
    )
    scaled = (grads.astype(jnp.float32)[:, None, :] * probs[:, :, None]).astype(jnp.bfloat16)
    scaled = scaled.reshape(tok_rows * TOPK, width)
    packed = jnp.dot(dispatch, scaled, preferred_element_type=jnp.float32).astype(jnp.bfloat16)
    packed = packed.reshape(EXPERTS, CAP, width)
    outgoing = jnp.broadcast_to(packed[:, None], (EXPERTS, slices, CAP, width)).reshape(
        EXPERTS * slices, CAP, width
    )
    return (outgoing, dispatch)


def expert_part(received, saved, gate_w, up_w, down_w):
    sources = received.shape[0]
    width = received.shape[2]
    rows = received.reshape(sources * CAP, width)
    hidden_grad = lax.dot_general(
        rows, down_w, (((1,), (1,)), ((), ())), preferred_element_type=jnp.float32
    )
    gate_pre = saved[:, 0, :].astype(jnp.float32)
    up_pre = saved[:, 1, :].astype(jnp.float32)
    sigmoid_gate = jax.nn.sigmoid(gate_pre)
    gate_grad = (
        hidden_grad * up_pre * sigmoid_gate * (1.0 + gate_pre * (1.0 - sigmoid_gate))
    ).astype(jnp.bfloat16)
    up_grad = (hidden_grad * gate_pre * sigmoid_gate).astype(jnp.bfloat16)
    partial_value = lax.dot_general(
        gate_grad, gate_w, (((1,), (1,)), ((), ())), preferred_element_type=jnp.float32
    )
    partial_value = partial_value + lax.dot_general(
        up_grad, up_w, (((1,), (1,)), ((), ())), preferred_element_type=jnp.float32
    )
    return partial_value.astype(jnp.bfloat16).reshape(sources, CAP, width)


def expert_work(received, saved, gate_w, up_w, down_w):
    return expert_part(received, saved, gate_w, up_w, down_w)


def send_out(outgoing):
    return lax.all_to_all(outgoing, "expert", split_axis=0, concat_axis=0, tiled=True)


def send_back(term):
    return lax.all_to_all(term, "expert", split_axis=0, concat_axis=0, tiled=True)


def combine(returned, dispatch, grads, slices):
    tok_rows = grads.shape[0]
    width = grads.shape[1]
    summed = jnp.sum(returned.reshape(EXPERTS, slices, CAP, width).astype(jnp.float32), axis=1)
    summed = summed.reshape(EXPERTS * CAP, width)
    per_route = lax.dot_general(
        dispatch.astype(jnp.float32),
        summed,
        (((0,), (0,)), ((), ())),
        precision=lax.Precision.HIGHEST,
        preferred_element_type=jnp.float32,
    )
    result = grads.astype(jnp.float32) + jnp.sum(per_route.reshape(tok_rows, TOPK, width), axis=1)
    return result.astype(jnp.bfloat16)


def per_device(
    held_a, held_b, new_a, new_b, expert_ids, route_probs, saved_gate_up, w_gate, w_up, w_down
):
    slices = lax.axis_size("expert") // EXPERTS
    gate_w = w_gate[0]
    up_w = w_up[0]
    down_w = w_down[0]

    def single_layer(grads, micro):
        outgoing, dispatch = route_layout(
            grads, expert_ids[0, micro], route_probs[0, micro], slices
        )
        received = send_out(outgoing)
        term = expert_work(received, saved_gate_up[0, micro], gate_w, up_w, down_w)
        returned = send_back(term)
        return combine(returned, dispatch, grads, slices)

    def paired_layers(grads_one, grads_two, micro_one, micro_two):
        return (single_layer(grads_one, micro_one), single_layer(grads_two, micro_two))

    first_a, first_b = paired_layers(held_a[0], held_b[0], 0, 1)
    section = lax.axis_index("pipe")
    shifted_a = passed_along(first_a, "pipe", -1)
    shifted_b = passed_along(first_b, "pipe", 1)
    into_a = jnp.where(section == lax.axis_size("pipe") - 1, new_a, shifted_a)
    into_b = jnp.where(section == 0, new_b, shifted_b)
    second_a, second_b = paired_layers(into_a, into_b, 2, 3)
    return (first_a[None], first_b[None], second_a[None], second_b[None])


def solution(mesh):
    in_specs = (
        P("pipe", "expert", None),
        P("pipe", "expert", None),
        P("expert", None),
        P("expert", None),
        P("pipe", None, "expert", None),
        P("pipe", None, "expert", None),
        P("pipe", None, None, None, "expert"),
        P("pipe", None, "expert"),
        P("pipe", None, "expert"),
        P("pipe", "expert", None),
    )
    out_specs = (
        P("pipe", "expert", None),
        P("pipe", "expert", None),
        P("pipe", "expert", None),
        P("pipe", "expert", None),
    )
    return jax.shard_map(
        per_device, mesh=mesh, in_specs=in_specs, out_specs=out_specs, check_vma=False
    )
```

profile of v0, /device:TPU:0, one launch (start us, length us, event | category | flops | bytes accessed | tf_op | source)
XLA Modules:
  0.0 919.7 jit_solution(14090318261672604463)
XLA Ops:
  14.0 9.6 %all-to-all-start = ((bf16[32,10,7168]{2,1,0:T(8,128)(2,1)}), bf16[32,10,7168]{2,1,0:T(8,128)(2,1)}, u32[]{:S(2)}, u32[]{:S(2)}) async-start(bf16[32,10,7168]{2,1,0:T(8,128)(2,1)} %bitcast.176), calls=%async_computation | async-start | bytes 14680064 | tf_op jit(solution)/shard_map/all_to_all | solution.py:65
  29.9 97.6 %all-to-all-done = bf16[32,10,7168]{2,1,0:T(8,128)(2,1)} async-done(((bf16[32,10,7168]{2,1,0:T(8,128)(2,1)}), bf16[32,10,7168]{2,1,0:T(8,128)(2,1)}, u32[]{:S(2)}, u32[]{:S(2)}) %all-to-all-start) | async-done | bytes 4587552 | tf_op jit(solution)/shard_map/all_to_all | solution.py:65
  131.6 7.9 all-to-all-start.2
  141.1 8.0 reshape.251
  149.1 5.0 fusion.22
  159.7 7.8 reshape.252
  167.5 64.2 %all-to-all-done.2 = bf16[32,10,7168]{2,1,0:T(8,128)(2,1)} async-done(((bf16[32,10,7168]{2,1,0:T(8,128)(2,1)}), bf16[32,10,7168]{2,1,0:T(8,128)(2,1)}, u32[]{:S(2)}, u32[]{:S(2)}) %all-to-all-start.2) | async-done | bytes 4587552 | tf_op jit(solution)/shard_map/all_to_all | solution.py:65
  231.6 11.0 %all-to-all-start.1 = ((bf16[32,10,7168]{2,1,0:T(8,128)(2,1)}), bf16[32,10,7168]{2,1,0:T(8,128)(2,1)}, u32[]{:S(2)}, u32[]{:S(2)}) async-start(bf16[32,10,7168]{2,1,0:T(8,128)(2,1)} %reshape.252), calls=%async_computation.1 | async-start | bytes 14680064 | tf_op jit(solution)/shard_map/all_to_all | solution.py:69
  245.9 8.0 reshape.255
  253.9 5.0 fusion.20
  264.5 7.9 reshape.256
  272.4 80.5 %all-to-all-done.1 = bf16[32,10,7168]{2,1,0:T(8,128)(2,1)} async-done(((bf16[32,10,7168]{2,1,0:T(8,128)(2,1)}), bf16[32,10,7168]{2,1,0:T(8,128)(2,1)}, u32[]{:S(2)}, u32[]{:S(2)}) %all-to-all-start.1) | async-done | bytes 4587552 | tf_op jit(solution)/shard_map/all_to_all | solution.py:69
  352.9 5.1 all-to-all-start.3
  358.1 6.6 convert_reduce_fusion.3
  382.2 71.9 %all-to-all-done.3 = bf16[32,10,7168]{2,1,0:T(8,128)(2,1)} async-done(((bf16[32,10,7168]{2,1,0:T(8,128)(2,1)}), bf16[32,10,7168]{2,1,0:T(8,128)(2,1)}, u32[]{:S(2)}, u32[]{:S(2)}) %all-to-all-start.3) | async-done | bytes 4587552 | tf_op jit(solution)/shard_map/all_to_all | solution.py:69
  458.1 11.3 %all-to-all-start.4 = ((bf16[32,10,7168]{2,1,0:T(8,128)(2,1)}), bf16[32,10,7168]{2,1,0:T(8,128)(2,1)}, u32[]{:S(2)}, u32[]{:S(2)}) async-start(bf16[32,10,7168]{2,1,0:T(8,128)(2,1)} %bitcast.175), calls=%async_computation.4 | async-start | bytes 14680064 | tf_op jit(solution)/shard_map/all_to_all | solution.py:65
  469.4 6.6 convert_reduce_fusion.2
  481.5 11.9 %collective-permute-start.1 = (bf16[32,7168]{1,0:T(8,128)(2,1)S(1)}, bf16[32,7168]{1,0:T(8,128)(2,1)S(1)}, u32[]{:S(2)}, u32[]{:S(2)}) collective-permute-start(bf16[32,7168]{1,0:T(8,128)(2,1)S(1)} %add_convert_fusion.1), channel_id=1, source_target_pairs={{0,32},{32,64},{64,96},{1,33},{33,65},{65,97},{2,34},{34,66},{66,9... | collective-permute-start | bytes 1376264 | tf_op jit(solution)/shard_map/ppermute | solution.py:14
  504.6 51.3 %all-to-all-done.4 = bf16[32,10,7168]{2,1,0:T(8,128)(2,1)} async-done(((bf16[32,10,7168]{2,1,0:T(8,128)(2,1)}), bf16[32,10,7168]{2,1,0:T(8,128)(2,1)}, u32[]{:S(2)}, u32[]{:S(2)}) %all-to-all-start.4) | async-done | bytes 4587552 | tf_op jit(solution)/shard_map/all_to_all | solution.py:65
  559.9 14.0 %all-to-all-start.6 = ((bf16[32,10,7168]{2,1,0:T(8,128)(2,1)}), bf16[32,10,7168]{2,1,0:T(8,128)(2,1)}, u32[]{:S(2)}, u32[]{:S(2)}) async-start(bf16[32,10,7168]{2,1,0:T(8,128)(2,1)} %bitcast.178), calls=%async_computation.6 | async-start | bytes 14680064 | tf_op jit(solution)/shard_map/all_to_all | solution.py:65
  574.0 8.0 reshape.259
  582.0 5.0 fusion.18
  592.5 7.8 reshape.260
  600.2 54.8 %all-to-all-done.6 = bf16[32,10,7168]{2,1,0:T(8,128)(2,1)} async-done(((bf16[32,10,7168]{2,1,0:T(8,128)(2,1)}), bf16[32,10,7168]{2,1,0:T(8,128)(2,1)}, u32[]{:S(2)}, u32[]{:S(2)}) %all-to-all-start.6) | async-done | bytes 4587552 | tf_op jit(solution)/shard_map/all_to_all | solution.py:65
  655.0 18.0 %all-to-all-start.5 = ((bf16[32,10,7168]{2,1,0:T(8,128)(2,1)}), bf16[32,10,7168]{2,1,0:T(8,128)(2,1)}, u32[]{:S(2)}, u32[]{:S(2)}) async-start(bf16[32,10,7168]{2,1,0:T(8,128)(2,1)} %reshape.260), calls=%async_computation.5 | async-start | bytes 14680064 | tf_op jit(solution)/shard_map/all_to_all | solution.py:69
  673.1 8.0 reshape.263
  691.7 7.8 reshape.264
  699.5 63.6 %all-to-all-done.5 = bf16[32,10,7168]{2,1,0:T(8,128)(2,1)} async-done(((bf16[32,10,7168]{2,1,0:T(8,128)(2,1)}), bf16[32,10,7168]{2,1,0:T(8,128)(2,1)}, u32[]{:S(2)}, u32[]{:S(2)}) %all-to-all-start.5) | async-done | bytes 4587552 | tf_op jit(solution)/shard_map/all_to_all | solution.py:69
  763.1 21.4 %all-to-all-start.7 = ((bf16[32,10,7168]{2,1,0:T(8,128)(2,1)}), bf16[32,10,7168]{2,1,0:T(8,128)(2,1)}, u32[]{:S(2)}, u32[]{:S(2)}) async-start(bf16[32,10,7168]{2,1,0:T(8,128)(2,1)} %reshape.264), calls=%async_computation.7 | async-start | bytes 14680064 | tf_op jit(solution)/shard_map/all_to_all | solution.py:69
  785.6 6.6 convert_reduce_fusion.1
  796.7 111.9 %all-to-all-done.7 = bf16[32,10,7168]{2,1,0:T(8,128)(2,1)} async-done(((bf16[32,10,7168]{2,1,0:T(8,128)(2,1)}), bf16[32,10,7168]{2,1,0:T(8,128)(2,1)}, u32[]{:S(2)}, u32[]{:S(2)}) %all-to-all-start.7) | async-done | bytes 4587552 | tf_op jit(solution)/shard_map/all_to_all | solution.py:69
  908.5 6.6 convert_reduce_fusion
  (143 shorter events, 107.8 us)
Async XLA Ops:
  14.0 10.2 %copy-start.15 = (bf16[1,32,7168]{2,1,0:T(8,128)(2,1)S(1)}, bf16[1,32,7168]{2,1,0:T(8,128)(2,1)}, u32[]{:S(2)}) copy-start(bf16[1,32,7168]{2,1,0:T(8,128)(2,1)} %param.11) | copy-start | bytes 1376260
  14.0 113.6 %all-to-all-start = ((bf16[32,10,7168]{2,1,0:T(8,128)(2,1)}), bf16[32,10,7168]{2,1,0:T(8,128)(2,1)}, u32[]{:S(2)}, u32[]{:S(2)}) async-start(bf16[32,10,7168]{2,1,0:T(8,128)(2,1)} %bitcast.176), calls=%async_computation | async-start | bytes 14680064 | tf_op jit(solution)/shard_map/all_to_all | solution.py:65
  131.6 7.9 copy-start.18
  131.6 100.1 %all-to-all-start.2 = ((bf16[32,10,7168]{2,1,0:T(8,128)(2,1)}), bf16[32,10,7168]{2,1,0:T(8,128)(2,1)}, u32[]{:S(2)}, u32[]{:S(2)}) async-start(bf16[32,10,7168]{2,1,0:T(8,128)(2,1)} %bitcast.177), calls=%async_computation.2 | async-start | bytes 14680064 | tf_op jit(solution)/shard_map/all_to_all | solution.py:65
  149.1 5.0 copy-start.4
  154.1 2.0 copy-start
  167.5 77.8 %copy-start.19 = (s32[1,4,32,2]{2,3,1,0:T(2,128)S(1)}, s32[1,4,32,2]{2,3,1,0:T(2,128)}, u32[]{:S(2)}) copy-start(s32[1,4,32,2]{2,3,1,0:T(2,128)} %param.14) | copy-start | bytes 3076
  231.6 121.3 %all-to-all-start.1 = ((bf16[32,10,7168]{2,1,0:T(8,128)(2,1)}), bf16[32,10,7168]{2,1,0:T(8,128)(2,1)}, u32[]{:S(2)}, u32[]{:S(2)}) async-start(bf16[32,10,7168]{2,1,0:T(8,128)(2,1)} %reshape.252), calls=%async_computation.1 | async-start | bytes 14680064 | tf_op jit(solution)/shard_map/all_to_all | solution.py:69
  244.7 0.6 copy-start.21
  253.9 5.0 copy-start.5
  258.9 2.0 copy-start.1
  352.9 101.2 %all-to-all-start.3 = ((bf16[32,10,7168]{2,1,0:T(8,128)(2,1)}), bf16[32,10,7168]{2,1,0:T(8,128)(2,1)}, u32[]{:S(2)}, u32[]{:S(2)}) async-start(bf16[32,10,7168]{2,1,0:T(8,128)(2,1)} %reshape.256), calls=%async_computation.3 | async-start | bytes 14680064 | tf_op jit(solution)/shard_map/all_to_all | solution.py:69
  369.9 3.7 collective-permute-start
  373.7 1.0 copy-start.10
  458.1 97.8 %all-to-all-start.4 = ((bf16[32,10,7168]{2,1,0:T(8,128)(2,1)}), bf16[32,10,7168]{2,1,0:T(8,128)(2,1)}, u32[]{:S(2)}, u32[]{:S(2)}) async-start(bf16[32,10,7168]{2,1,0:T(8,128)(2,1)} %bitcast.175), calls=%async_computation.4 | async-start | bytes 14680064 | tf_op jit(solution)/shard_map/all_to_all | solution.py:65
  476.0 2.2 copy-start.20
  479.5 0.9 copy-start.8
  481.5 13.4 %collective-permute-start.1 = (bf16[32,7168]{1,0:T(8,128)(2,1)S(1)}, bf16[32,7168]{1,0:T(8,128)(2,1)S(1)}, u32[]{:S(2)}, u32[]{:S(2)}) collective-permute-start(bf16[32,7168]{1,0:T(8,128)(2,1)S(1)} %add_convert_fusion.1), channel_id=1, source_target_pairs={{0,32},{32,64},{64,96},{1,33},{33,65},{65,97},{2,34},{34,66},{66,9... | collective-permute-start | bytes 1376264 | tf_op jit(solution)/shard_map/ppermute | solution.py:14
  496.1 0.9 copy-start.12
  559.9 14.0 %copy-start.17 = (bf16[1,1,320,2,256]{4,3,2,1,0:T(2,128)(2,1)S(1)}, bf16[1,1,320,2,256]{4,3,2,1,0:T(2,128)(2,1)}, u32[]{:S(2)}) copy-start(bf16[1,1,320,2,256]{4,3,2,1,0:T(2,128)(2,1)} %get-tuple-element.5) | copy-start | bytes 983044
  559.9 95.2 %all-to-all-start.6 = ((bf16[32,10,7168]{2,1,0:T(8,128)(2,1)}), bf16[32,10,7168]{2,1,0:T(8,128)(2,1)}, u32[]{:S(2)}, u32[]{:S(2)}) async-start(bf16[32,10,7168]{2,1,0:T(8,128)(2,1)} %bitcast.178), calls=%async_computation.6 | async-start | bytes 14680064 | tf_op jit(solution)/shard_map/all_to_all | solution.py:65
  582.0 5.0 copy-start.6
  587.0 2.0 copy-start.2
  655.0 108.0 %all-to-all-start.5 = ((bf16[32,10,7168]{2,1,0:T(8,128)(2,1)}), bf16[32,10,7168]{2,1,0:T(8,128)(2,1)}, u32[]{:S(2)}, u32[]{:S(2)}) async-start(bf16[32,10,7168]{2,1,0:T(8,128)(2,1)} %reshape.260), calls=%async_computation.5 | async-start | bytes 14680064 | tf_op jit(solution)/shard_map/all_to_all | solution.py:69
  681.2 5.0 copy-start.7
  686.1 2.0 copy-start.3
  699.5 85.0 %copy-start.9 = (f32[32,7168]{1,0:T(8,128)S(1)}, f32[32,7168]{1,0:T(8,128)}, u32[]{:S(2)}) copy-start(f32[32,7168]{1,0:T(8,128)} %copy-done.8) | copy-start | bytes 2752516
  699.5 85.0 %copy-start.14 = (bf16[1,32,7168]{2,1,0:T(8,128)(2,1)S(1)}, bf16[1,32,7168]{2,1,0:T(8,128)(2,1)}, u32[]{:S(2)}) copy-start(bf16[1,32,7168]{2,1,0:T(8,128)(2,1)} %param.10) | copy-start | bytes 1376260
  699.5 85.0 %copy-start.16 = (bf16[1,32,7168]{2,1,0:T(8,128)(2,1)S(1)}, bf16[1,32,7168]{2,1,0:T(8,128)(2,1)}, u32[]{:S(2)}) copy-start(bf16[1,32,7168]{2,1,0:T(8,128)(2,1)} %param.11) | copy-start | bytes 1376260
  763.1 145.4 %all-to-all-start.7 = ((bf16[32,10,7168]{2,1,0:T(8,128)(2,1)}), bf16[32,10,7168]{2,1,0:T(8,128)(2,1)}, u32[]{:S(2)}, u32[]{:S(2)}) async-start(bf16[32,10,7168]{2,1,0:T(8,128)(2,1)} %reshape.264), calls=%async_computation.7 | async-start | bytes 14680064 | tf_op jit(solution)/shard_map/all_to_all | solution.py:69
  792.2 3.5 copy-start.11
  915.1 3.5 copy-start.13
  (1 other events, 0.6 us)
where the time goes:
time: 930 us; the launch traced here: 920 us
  waiting for transfers between devices  597 us (64%)
  local copies, waits for them, and re-layouts  124 us (13%)
  starting transfers between devices  111 us (12%)
  matrix products  49.4 us (5%)
  other arithmetic  37.1 us (4%)
    all_to_all x4, waiting for transfers between devices, send_back(): lax.all_to_all(term, 'expert', split_axis=0, concat_axis=0, tiled=True)  328 us
    all_to_all x4, waiting for transfers between devices, send_out(): lax.all_to_all(outgoing, 'expert', split_axis=0, concat_axis=0, tiled=True)  268 us
    all_to_all x4, starting transfers between devices, send_back(): lax.all_to_all(term, 'expert', split_axis=0, concat_axis=0, tiled=True)  55.6 us
    all_to_all x4, starting transfers between devices, send_out(): lax.all_to_all(outgoing, 'expert', split_axis=0, concat_axis=0, tiled=True)  42.7 us
    reshape x4, local copies, waits for them, and re-layouts, expert_part(): rows = received.reshape(sources * CAP, width)  32.1 us
    reshape x4, local copies, waits for them, and re-layouts, expert_part(): return partial_value.astype(jnp.bfloat16).reshape(sources, CAP, width)  31.2 us
    reduce_sum x4, other arithmetic, combine(): jnp.sum(returned.reshape(EXPERTS, slices, CAP, width).astype(jnp.float32)...  26.4 us
    broadcast_in_dim x8, local copies, waits for them, and re-layouts, route_layout(): jnp.broadcast_to(packed[:, None], (EXPERTS, slices, CAP, width))  20 us
  transfers between devices with their start and end apart: 10, of which 9 were waited for; matrix products, arithmetic and copies ran while one was open for 18% of the time, Pallas kernels for 0%

commit v1 on v0

v1 whole, which is shorter than its diff:
```python
import functools

import jax
import jax.numpy as jnp
import numpy as np
from jax import lax
from jax.experimental import pallas as pl
from jax.experimental.pallas import tpu as pltpu
from jax.sharding import PartitionSpec as P

EXPERTS = 8
TOPK = 2
CAP = 10
D = 7168
TOK = 32
HD = 256
NX, NY, NZ = 2, 4, 4
ROWS = NX * NY * NZ * CAP
BLK = ROWS // 4
PADY = 32
NCH = 7
CW = D // NCH
C1 = 640
C3 = CW - C1
HA = 48
RING = 3
SLOTS_PHASE = 4 * NCH
UNITS = 2 * SLOTS_PHASE
MESH = pl.DeviceIdType.MESH
F32, BF16 = jnp.float32, jnp.bfloat16

X1, Y1, Z3A, Z3B, Z1A, Z1F, X3, Y3 = 0, 1, 4, 6, 8, 10, 12, 13
R1A, Y3R, R1B, X3R, Y1R, R3A, X1R, R3B, PIPE = 16, 18, 21, 23, 24, 27, 29, 30, 32
KINDS = 34


def constants():
    c = np.arange(CAP)
    order1 = np.array(
        [(x, y, z, k) for z in range(NZ) for y in range(NY) for x in range(NX) for k in c]
    )
    order3 = np.array(
        [(x, y, z, k) for y in range(NY) for x in range(NX) for z in range(NZ) for k in c]
    )
    row = lambda o: ((o[:, 0] * NY + o[:, 1]) * NZ + o[:, 2]) * CAP + o[:, 3]
    row1, row3 = row(order1), row(order3)
    from3 = (row1[:, None] == row3[None, :]).astype(np.float32)
    from_saved = (row1[:, None] == np.arange(ROWS)[None, :]).astype(np.float32)
    want3 = (order3[:, 0] * NZ + order3[:, 2]) * 128 + order3[:, 1] * CAP + order3[:, 3]
    want1 = np.full((NY * PADY,), -(1 << 20))
    pick = np.zeros((BLK, NY * PADY), np.float32)
    for y in range(NY):
        for x in range(NX):
            for k in c:
                want1[y * PADY + x * CAP + k] = x * 128 + y * CAP + k
                pick[(y * NX + x) * CAP + k, y * PADY + x * CAP + k] = 1
    lane = np.zeros((1, 128), np.float32)
    lane[0] = np.arange(128) // TOK
    off3 = (np.arange(NX * NZ * TOK) // TOK) * 128
    f = lambda a: np.asarray(a, np.float32)
    b = lambda a: np.asarray(a, np.float32).astype(jnp.bfloat16)
    return (
        b(from3),
        b(from3.T),
        b(from_saved),
        b(pick),
        b(pick.T),
        f(want3)[:, None],
        f(want3)[None, :],
        f(want1)[:, None],
        f(want1)[None, :],
        f(off3)[:, None],
        f(off3)[None, :],
        lane,
    )


def dot(a, b):
    return lax.dot_general(a, b, (((1,), (0,)), ((), ())), preferred_element_type=F32)


def dot_t(a, b):
    return lax.dot_general(a, b, (((1,), (1,)), ((), ())), preferred_element_type=F32)


def kernel(
    xa_ref, xb_ref, na_ref, nb_ref, meta_ref, saved_ref, wg_ref, wu_ref, wdn_ref,
    from3_ref, to3_ref, froms_ref, pick_ref, spread_ref,
    w3c_ref, w3r_ref, w1c_ref, w1r_ref, o3c_ref, o3r_ref, lane_ref,
    out_ref,
    xin, wgu, wd, svd, mr, a1, a1t, pr1, a3, a3t, pr3, fg, fu, acc1, acc3, gu1, gu3,
    t1, y1, z1, t3, y3, y1s, y3s,
    q1, s1, r1a, r1b, y1rs, y1rr, tb1, x1r, q3, y3r, tb3, x3r, v3, s3, r3a, r3b,
    ss, rs, mss, mrs, ls,
):
    me = lax.axis_index("expert")
    pp = lax.axis_index("pipe")
    x, y, z = me // (NY * NZ), (me // NZ) % NY, me % NZ
    core = pp % 2
    xn = 1 - x
    za = (z + 1 + 2 * core) % NZ
    zb = (z + 3 - 2 * core) % NZ
    z2 = (z + 2) % NZ

    def dev(px, py, pz):
        return {"expert": (px * NY + py) * NZ + pz}

    def rcopy(src, dst, kind, g, c, to):
        return pltpu.make_async_remote_copy(
            src_ref=src, dst_ref=dst, send_sem=ss.at[g % RING, kind], recv_sem=rs.at[c, kind],
            device_id=to, device_id_type=MESH,
        )

    def finish(src, landing, kind, g, c, to):
        d = rcopy(src, landing, kind, g, c, to)
        d.wait_send()
        d.wait_recv()

    def load(src, dst, k):
        return pltpu.make_async_copy(src, dst, ls.at[k])

    load(xa_ref, xin.at[0], 0).start()
    load(xb_ref, xin.at[1], 1).start()

    @pl.when(pp == 3)
    def _():
        load(na_ref, xin.at[2], 2).start()

    @pl.when(pp == 0)
    def _():
        load(nb_ref, xin.at[3], 3).start()

    load(saved_ref, svd, 4).start()
    load(wdn_ref, wd, 5).start()
    load(wg_ref, wgu.at[:, 0:HD], 6).start()
    load(wu_ref, wgu.at[:, HD:2 * HD], 7).start()

    barrier = pltpu.get_barrier_semaphore()
    metas = [(dx, dz) for dx in range(NX) for dz in range(NZ) if dx or dz]
    for dx, dz in metas:
        pl.semaphore_signal(barrier, 1, device_id=dev((x + dx) % NX, y, (z + dz) % NZ), device_id_type=MESH)
    for dy in range(1, NY):
        pl.semaphore_signal(barrier, 1, device_id=dev(x, (y + dy) % NY, z), device_id_type=MESH)

    @pl.when(pp > 0)
    def _():
        pl.semaphore_signal(barrier, 1, device_id={"pipe": pp - 1}, device_id_type=MESH)

    @pl.when(pp < 3)
    def _():
        pl.semaphore_signal(barrier, 1, device_id={"pipe": pp + 1}, device_id_type=MESH)

    in_pipe = jnp.where((pp == 0) | (pp == 3), 1, 2)
    pl.semaphore_wait(barrier, len(metas) + NY - 1 + in_pipe)

    src_me = x * NZ + z
    mr[src_me] = meta_ref[...]

    def meta_copy(k, dx, dz, landing):
        return pltpu.make_async_remote_copy(
            src_ref=meta_ref, dst_ref=mr.at[landing], send_sem=mss.at[k], recv_sem=mrs.at[k],
            device_id=dev((x + dx) % NX, y, (z + dz) % NZ), device_id_type=MESH,
        )

    for k, (dx, dz) in enumerate(metas):
        meta_copy(k, dx, dz, src_me).start()

    load(xa_ref, xin.at[0], 0).wait()
    load(xb_ref, xin.at[1], 1).wait()

    @pl.when(pp == 3)
    def _():
        load(na_ref, xin.at[2], 2).wait()

    @pl.when(pp == 0)
    def _():
        load(nb_ref, xin.at[3], 3).wait()

    def col(c, off, width):
        return pl.ds(pl.multiple_of(c * CW + off, 128), width)

    def routes(st, m):
        lane = lane_ref[...]

        def rowpart(s):
            return mr[s, pl.ds(pl.multiple_of(m * 8, 8), 8), :]

        def colpart(s):
            return mr[s, 32:64, :]

        def lanes(parts):
            r = parts[-1]
            for i in range(len(parts) - 2, -1, -1):
                r = jnp.where(lane == float(i), parts[i], r)
            return r

        lane_no = lax.broadcasted_iota(jnp.int32, (1, 128), 1)

        def column(arr, k):
            return jnp.sum(jnp.where(lane_no == m * 4 + k, arr, 0.0), axis=1, keepdims=True)

        mine = (x * 40).astype(F32)
        r1 = lanes([rowpart(z), rowpart(NZ + z)])[:, :NX * TOK]
        o1 = o3r_ref[:, :NX * TOK]
        w1 = w1c_ref[...] + mine
        h0, h1 = w1 == r1[0:1] + o1, w1 == r1[1:2] + o1
        a1[st] = jnp.where(h0 | h1, 1.0, 0.0).astype(BF16)
        pr1[st] = jnp.sum(jnp.where(h0, r1[2:3], 0.0) + jnp.where(h1, r1[3:4], 0.0), axis=1, keepdims=True)
        c1 = jnp.concatenate([colpart(z), colpart(NZ + z)], axis=0)
        o1c = o3c_ref[:NX * TOK, :]
        w1t = w1r_ref[...] + mine
        a1t[st] = jnp.where(
            (column(c1, 0) + o1c == w1t) | (column(c1, 1) + o1c == w1t), 1.0, 0.0
        ).astype(BF16)
        r3 = jnp.concatenate([lanes([rowpart(s) for s in range(4)]), lanes([rowpart(s) for s in range(4, 8)])], axis=1)
        o3 = o3r_ref[...]
        w3 = w3c_ref[...] + mine
        h0, h1 = w3 == r3[0:1] + o3, w3 == r3[1:2] + o3
        a3[st] = jnp.where(h0 | h1, 1.0, 0.0).astype(BF16)
        pr3[st] = jnp.sum(jnp.where(h0, r3[2:3], 0.0) + jnp.where(h1, r3[3:4], 0.0), axis=1, keepdims=True)
        c3 = mr[:, 32:64, :].reshape(NX * NZ * TOK, 128)
        o3t = o3c_ref[...]
        w3t = w3r_ref[...] + mine
        a3t[st] = jnp.where(
            (column(c3, 0) + o3t == w3t) | (column(c3, 1) + o3t == w3t), 1.0, 0.0
        ).astype(BF16)

    def factors(st, m):
        gu = dot(froms_ref[...], svd[m])
        gate, up = gu[:, :HD], gu[:, HD:]
        sig = jax.nn.sigmoid(gate)
        fg[st] = up * sig * (1.0 + gate * (1.0 - sig))
        fu[st] = gate * sig

    def to_y(src_of, buf, st, c, g, kind):
        for dy in range(1, NY):
            yd = (y + dy) % NY
            rcopy(src_of(yd), buf.at[st, c, y], kind + dy - 1, g, c, dev(x, yd, z)).start()

    def from_y(src_of, buf, st, c, g, kind):
        for dy in range(1, NY):
            yd, ys = (y + dy) % NY, (y - dy + NY) % NY
            finish(src_of(yd), buf.at[st, c, ys], kind + dy - 1, g, c, dev(x, yd, z))

    def d0(p, st, c, g):
        m = 2 * p + st

        @pl.when((p == 1) & (((st == 0) & (pp < 3)) | ((st == 1) & (pp > 0))))
        def _():
            landing = xin.at[m, :, col(c, 0, CW)]
            rcopy(landing, landing, PIPE + st, g, c, {"pipe": pp}).wait_recv()

        t1[st, c, x] = xin[m, :, col(c, 0, C1)]
        rcopy(t1.at[st, c, x], t1.at[st, c, x], X1, g, c, dev(xn, y, z)).start()
        t3[st, c, x, z] = xin[m, :, col(c, C1, C3)]
        mine = t3.at[st, c, x, z]
        rcopy(mine, mine, Z3A, g, c, dev(x, y, za)).start()
        rcopy(mine, mine, Z3A + 1, g, c, dev(x, y, zb)).start()

        @pl.when(c == 0)
        def _():
            @pl.when(g == 0)
            def _():
                for k, (dx, dz) in enumerate(metas):
                    landing = ((x + dx) % NX) * NZ + (z - dz + NZ) % NZ
                    d = meta_copy(k, dx, dz, landing)
                    d.wait_send()
                    d.wait_recv()

            routes(st, m)

    def d1(p, st, c, g):
        finish(t1.at[st, c, x], t1.at[st, c, xn], X1, g, c, dev(xn, y, z))
        rows = dot(a1[st], t1[st, c].reshape(NX * TOK, C1)) * pr1[st]
        ring = g % RING
        y1s[ring] = rows.astype(BF16).reshape(NY, PADY, C1)
        to_y(lambda yd: y1s.at[ring, yd], y1, st, c, g, Y1)
        y1[st, c, y] = y1s[ring, y]
        mine = t3.at[st, c, x, z]
        finish(mine, t3.at[st, c, x, zb], Z3A, g, c, dev(x, y, za))
        finish(mine, t3.at[st, c, x, za], Z3A + 1, g, c, dev(x, y, zb))
        fwd_a, fwd_b = t3.at[st, c, x, zb, 0:16], t3.at[st, c, x, za, 16:32]
        rcopy(fwd_a, fwd_a, Z3B, g, c, dev(x, y, za)).start()
        rcopy(fwd_b, fwd_b, Z3B + 1, g, c, dev(x, y, zb)).start()

    def d2(p, st, c, g):
        ring = g % RING
        from_y(lambda yd: y1s.at[ring, yd], y1, st, c, g, Y1)
        z1[st, c, z] = dot(pick_ref[...], y1[st, c].reshape(NY * PADY, C1)).astype(BF16)
        mine = z1.at[st, c, z]
        rcopy(mine, mine, Z1A, g, c, dev(x, y, za)).start()
        rcopy(mine, mine, Z1A + 1, g, c, dev(x, y, zb)).start()
        finish(t3.at[st, c, x, zb, 0:16], t3.at[st, c, x, z2, 0:16], Z3B, g, c, dev(x, y, za))
        finish(t3.at[st, c, x, za, 16:32], t3.at[st, c, x, z2, 16:32], Z3B + 1, g, c, dev(x, y, zb))
        rcopy(t3.at[st, c, x], t3.at[st, c, x], X3, g, c, dev(xn, y, z)).start()

        @pl.when(c == 0)
        def _():
            @pl.when(g == 0)
            def _():
                load(saved_ref, svd, 4).wait()

            factors(st, 2 * p + st)

    def d3(p, st, c, g):
        ring = g % RING
        mine = z1.at[st, c, z]
        finish(mine, z1.at[st, c, zb], Z1A, g, c, dev(x, y, za))
        finish(mine, z1.at[st, c, za], Z1A + 1, g, c, dev(x, y, zb))
        fwd_a, fwd_b = z1.at[st, c, zb, 0:HA], z1.at[st, c, za, HA:BLK]
        rcopy(fwd_a, fwd_a, Z1F, g, c, dev(x, y, za)).start()
        rcopy(fwd_b, fwd_b, Z1F + 1, g, c, dev(x, y, zb)).start()
        finish(t3.at[st, c, x], t3.at[st, c, xn], X3, g, c, dev(xn, y, z))
        rows = dot(a3[st], t3[st, c].reshape(NX * NZ * TOK, C3)) * pr3[st]
        y3s[ring] = rows.astype(BF16).reshape(NY, BLK, C3)
        to_y(lambda yd: y3s.at[ring, yd], y3, st, c, g, Y3)
        y3[st, c, y] = y3s[ring, y]

    def d4(p, st, c, g):
        ring = g % RING
        finish(z1.at[st, c, zb, 0:HA], z1.at[st, c, z2, 0:HA], Z1F, g, c, dev(x, y, za))
        finish(z1.at[st, c, za, HA:BLK], z1.at[st, c, z2, HA:BLK], Z1F + 1, g, c, dev(x, y, zb))
        from_y(lambda yd: y3s.at[ring, yd], y3, st, c, g, Y3)

        @pl.when(g == 0)
        def _():
            load(wdn_ref, wd, 5).wait()

        h1 = dot_t(z1[st, c].reshape(ROWS, C1), wd[:, col(c, 0, C1)])
        h3 = dot_t(y3[st, c].reshape(ROWS, C3), wd[:, col(c, C1, C3)])

        @pl.when(c == 0)
        def _():
            acc1[st] = h1
            acc3[st] = h3

        @pl.when(c > 0)
        def _():
            acc1[st] += h1
            acc3[st] += h3

        @pl.when(c == NCH - 1)
        def _():
            other = acc3[st]
            high = other.astype(BF16)
            low = (other - high.astype(F32)).astype(BF16)
            h = acc1[st] + dot(from3_ref[...], high) + dot(from3_ref[...], low)
            gu1[st, :, 0:HD] = (h * fg[st]).astype(BF16)
            gu1[st, :, HD:2 * HD] = (h * fu[st]).astype(BF16)
            gu3[st] = dot(to3_ref[...], gu1[st]).astype(BF16)

    def r0(p, st, c, g):
        ring = g % RING

        @pl.when(g == 2 * NCH)
        def _():
            load(wg_ref, wgu.at[:, 0:HD], 6).wait()
            load(wu_ref, wgu.at[:, HD:2 * HD], 7).wait()

        part1 = dot_t(gu1[st], wgu[pl.ds(pl.multiple_of(c * CW, 128), C1), :])
        q1[ring] = part1.astype(BF16).reshape(NZ, BLK, C1)
        rcopy(q1.at[ring, z2, 0:HA], r1a.at[st, c, 0:HA], R1A, g, c, dev(x, y, za)).start()
        rcopy(q1.at[ring, z2, HA:BLK], r1a.at[st, c, HA:BLK], R1A + 1, g, c, dev(x, y, zb)).start()
        part3 = dot_t(gu3[st], wgu[pl.ds(pl.multiple_of(c * CW + C1, 128), C3), :])
        q3[ring] = part3.astype(BF16).reshape(NY, BLK, C3)
        to_y(lambda yd: q3.at[ring, yd], y3r, st, c, g, Y3R)
        y3r[st, c, y] = q3[ring, y]

    def r1(p, st, c, g):
        ring = g % RING
        finish(q1.at[ring, z2, 0:HA], r1a.at[st, c, 0:HA], R1A, g, c, dev(x, y, za))
        finish(q1.at[ring, z2, HA:BLK], r1a.at[st, c, HA:BLK], R1A + 1, g, c, dev(x, y, zb))
        s1[ring, 0, 0:HA] = (q1[ring, za, 0:HA].astype(F32) + r1a[st, c, 0:HA].astype(F32)).astype(BF16)
        s1[ring, 0, HA:BLK] = q1[ring, za, HA:BLK]
        rcopy(s1.at[ring, 0], r1b.at[st, c, 0], R1B, g, c, dev(x, y, za)).start()
        s1[ring, 1, 0:HA] = q1[ring, zb, 0:HA]
        s1[ring, 1, HA:BLK] = (q1[ring, zb, HA:BLK].astype(F32) + r1a[st, c, HA:BLK].astype(F32)).astype(BF16)
        rcopy(s1.at[ring, 1], r1b.at[st, c, 1], R1B + 1, g, c, dev(x, y, zb)).start()
        from_y(lambda yd: q3.at[ring, yd], y3r, st, c, g, Y3R)
        sums = dot(a3t[st], y3r[st, c].reshape(ROWS, C3))
        tb3[ring] = sums.astype(BF16).reshape(NX, NZ * TOK, C3)
        rcopy(tb3.at[ring, xn], x3r.at[st, c], X3R, g, c, dev(xn, y, z)).start()

    def r2(p, st, c, g):
        ring = g % RING
        finish(s1.at[ring, 0], r1b.at[st, c, 0], R1B, g, c, dev(x, y, za))
        finish(s1.at[ring, 1], r1b.at[st, c, 1], R1B + 1, g, c, dev(x, y, zb))
        total = q1[ring, z].astype(F32) + r1b[st, c, 0].astype(F32) + r1b[st, c, 1].astype(F32)
        rows = dot(spread_ref[...], total.astype(BF16))
        y1rs[ring] = rows.astype(BF16).reshape(NY, PADY, C1)
        to_y(lambda yd: y1rs.at[ring, yd], y1rr, st, c, g, Y1R)
        y1rr[st, c, y] = y1rs[ring, y]
        finish(tb3.at[ring, xn], x3r.at[st, c], X3R, g, c, dev(xn, y, z))
        v = tb3[ring, x].astype(F32) + x3r[st, c].astype(F32)
        v3[ring] = v.astype(BF16).reshape(NZ, TOK, C3)
        rcopy(v3.at[ring, z2, 0:16], r3a.at[st, c, 0:16], R3A, g, c, dev(x, y, za)).start()
        rcopy(v3.at[ring, z2, 16:32], r3a.at[st, c, 16:32], R3A + 1, g, c, dev(x, y, zb)).start()

    def r3(p, st, c, g):
        ring = g % RING
        from_y(lambda yd: y1rs.at[ring, yd], y1rr, st, c, g, Y1R)
        sums = dot(a1t[st], y1rr[st, c].reshape(NY * PADY, C1))
        tb1[ring] = sums.astype(BF16).reshape(NX, TOK, C1)
        rcopy(tb1.at[ring, xn], x1r.at[st, c], X1R, g, c, dev(xn, y, z)).start()
        finish(v3.at[ring, z2, 0:16], r3a.at[st, c, 0:16], R3A, g, c, dev(x, y, za))
        finish(v3.at[ring, z2, 16:32], r3a.at[st, c, 16:32], R3A + 1, g, c, dev(x, y, zb))
        s3[ring, 0, 0:16] = (v3[ring, za, 0:16].astype(F32) + r3a[st, c, 0:16].astype(F32)).astype(BF16)
        s3[ring, 0, 16:32] = v3[ring, za, 16:32]
        rcopy(s3.at[ring, 0], r3b.at[st, c, 0], R3B, g, c, dev(x, y, za)).start()
        s3[ring, 1, 0:16] = v3[ring, zb, 0:16]
        s3[ring, 1, 16:32] = (v3[ring, zb, 16:32].astype(F32) + r3a[st, c, 16:32].astype(F32)).astype(BF16)
        rcopy(s3.at[ring, 1], r3b.at[st, c, 1], R3B + 1, g, c, dev(x, y, zb)).start()

    def pipe_copy(m, st, c, g, to):
        cols = col(c, 0, CW)
        return rcopy(out_ref.at[m, :, cols], xin.at[m + 2, :, cols], PIPE + st, g, c, {"pipe": to})

    def r4(p, st, c, g):
        ring = g % RING
        m = 2 * p + st
        finish(tb1.at[ring, xn], x1r.at[st, c], X1R, g, c, dev(xn, y, z))
        finish(s3.at[ring, 0], r3b.at[st, c, 0], R3B, g, c, dev(x, y, za))
        finish(s3.at[ring, 1], r3b.at[st, c, 1], R3B + 1, g, c, dev(x, y, zb))
        cols1, cols3 = col(c, 0, C1), col(c, C1, C3)
        o1 = xin[m, :, cols1].astype(F32) + (tb1[ring, x].astype(F32) + x1r[st, c].astype(F32))
        out_ref[m, :, cols1] = o1.astype(BF16)
        o3 = xin[m, :, cols3].astype(F32) + (
            v3[ring, z].astype(F32) + r3b[st, c, 0].astype(F32) + r3b[st, c, 1].astype(F32)
        )
        out_ref[m, :, cols3] = o3.astype(BF16)

        @pl.when((p == 0) & (st == 0) & (pp > 0))
        def _():
            pipe_copy(0, 0, c, g, pp - 1).start()

        @pl.when((p == 0) & (st == 1) & (pp < 3))
        def _():
            pipe_copy(1, 1, c, g, pp + 1).start()

    def r5(p, st, c, g):
        @pl.when((p == 0) & (st == 0) & (pp > 0))
        def _():
            pipe_copy(0, 0, c, g, pp - 1).wait_send()

        @pl.when((p == 0) & (st == 1) & (pp < 3))
        def _():
            pipe_copy(1, 1, c, g, pp + 1).wait_send()

    def stage(t, k, returning, body):
        g = jnp.maximum(t - k, 0)
        p, w = g // SLOTS_PHASE, g % SLOTS_PHASE
        inside = (t - k >= 0) & (t - k < UNITS)
        here = (w >= 2 * NCH) if returning else (w < 2 * NCH)

        @pl.when(inside & here)
        def _():
            body(p, (w // NCH) % 2, w % NCH, g)

    def tick(t, carry):
        for k, body in enumerate([d0, d1, d2, d3, d4]):
            stage(t, k, False, body)
        for k, body in enumerate([r0, r1, r2, r3, r4, r5]):
            stage(t, k, True, body)
        return carry

    lax.fori_loop(0, UNITS + 5, tick, 0)


def layers(xa, xb, na, nb, meta, saved, wg, wu, wdn):
    consts = [jnp.asarray(a) for a in constants()]
    any_spec = pl.BlockSpec(memory_space=pl.ANY)
    vmem = pl.BlockSpec(memory_space=pltpu.VMEM)
    V = pltpu.VMEM
    scratch = [
        V((4, TOK, D), BF16),
        V((D, 2 * HD), BF16),
        V((HD, D), BF16),
        V((4, ROWS, 2 * HD), BF16),
        V((NX * NZ, 64, 128), F32),
        V((2, NY * PADY, NX * TOK), BF16),
        V((2, NX * TOK, NY * PADY), BF16),
        V((2, NY * PADY, 1), F32),
        V((2, ROWS, NX * NZ * TOK), BF16),
        V((2, NX * NZ * TOK, ROWS), BF16),
        V((2, ROWS, 1), F32),
        V((2, ROWS, HD), F32),
        V((2, ROWS, HD), F32),
        V((2, ROWS, HD), F32),
        V((2, ROWS, HD), F32),
        V((2, ROWS, 2 * HD), BF16),
        V((2, ROWS, 2 * HD), BF16),
        V((2, NCH, NX, TOK, C1), BF16),
        V((2, NCH, NY, PADY, C1), BF16),
        V((2, NCH, NZ, BLK, C1), BF16),
        V((2, NCH, NX, NZ, TOK, C3), BF16),
        V((2, NCH, NY, BLK, C3), BF16),
        V((RING, NY, PADY, C1), BF16),
        V((RING, NY, BLK, C3), BF16),
        V((RING, NZ, BLK, C1), BF16),
        V((RING, 2, BLK, C1), BF16),
        V((2, NCH, BLK, C1), BF16),
        V((2, NCH, 2, BLK, C1), BF16),
        V((RING, NY, PADY, C1), BF16),
        V((2, NCH, NY, PADY, C1), BF16),
        V((RING, NX, TOK, C1), BF16),
        V((2, NCH, TOK, C1), BF16),
        V((RING, NY, BLK, C3), BF16),
        V((2, NCH, NY, BLK, C3), BF16),
        V((RING, NX, NZ * TOK, C3), BF16),
        V((2, NCH, NZ * TOK, C3), BF16),
        V((RING, NZ, TOK, C3), BF16),
        V((RING, 2, TOK, C3), BF16),
        V((2, NCH, TOK, C3), BF16),
        V((2, NCH, 2, TOK, C3), BF16),
        pltpu.SemaphoreType.DMA((RING, KINDS)),
        pltpu.SemaphoreType.DMA((NCH, KINDS)),
        pltpu.SemaphoreType.DMA((8,)),
        pltpu.SemaphoreType.DMA((8,)),
        pltpu.SemaphoreType.DMA((8,)),
    ]
    flops = 4 * 2 * ROWS * D * HD * 3
    return pl.pallas_call(
        kernel,
        out_shape=jax.ShapeDtypeStruct((4, TOK, D), BF16),
        in_specs=[any_spec] * 4 + [vmem] + [any_spec] * 4 + [vmem] * len(consts),
        out_specs=vmem,
        scratch_shapes=scratch,
        compiler_params=pltpu.CompilerParams(
            collective_id=0, has_side_effects=True, vmem_limit_bytes=63 * 2**20
        ),
        cost_estimate=pl.CostEstimate(flops=flops, bytes_accessed=16 * 2**20, transcendentals=0),
        name="relay_layers",
    )(xa, xb, na, nb, meta, saved, wg, wu, wdn, *consts)


def route_data(ids, probs):
    micro = ids.shape[0]
    flat = ids.reshape(micro, TOK * TOPK)
    onehot = (flat[:, :, None] == jnp.arange(EXPERTS, dtype=jnp.int32)).astype(jnp.int32)
    ranking = jnp.sum((jnp.cumsum(onehot, axis=1) - 1) * onehot, axis=2)
    slots = (flat * CAP + ranking).reshape(micro, TOK, TOPK).astype(F32)
    both = jnp.concatenate([slots, probs], axis=2)
    by_row = jnp.tile(both.transpose(0, 2, 1), (1, 1, 128 // TOK))
    by_row = jnp.pad(by_row, ((0, 0), (0, 4), (0, 0))).reshape(micro * 8, 128)
    by_col = both.transpose(1, 0, 2).reshape(TOK, micro * 4)
    by_col = jnp.pad(by_col, ((0, 0), (0, 128 - micro * 4)))
    return jnp.concatenate([by_row, by_col], axis=0)


def per_device(
    held_a, held_b, new_a, new_b, expert_ids, route_probs, saved_gate_up, w_gate, w_up, w_down
):
    meta = route_data(expert_ids[0], route_probs[0])
    saved = saved_gate_up[0].reshape(4, ROWS, 2 * HD)
    out = layers(
        held_a[0], held_b[0], new_a, new_b, meta, saved, w_gate[0], w_up[0], w_down[0]
    )
    return out[0][None], out[1][None], out[2][None], out[3][None]


def solution(mesh):
    in_specs = (
        P("pipe", "expert", None),
        P("pipe", "expert", None),
        P("expert", None),
        P("expert", None),
        P("pipe", None, "expert", None),
        P("pipe", None, "expert", None),
        P("pipe", None, None, None, "expert"),
        P("pipe", None, "expert"),
        P("pipe", None, "expert"),
        P("pipe", "expert", None),
    )
    out_specs = (P("pipe", "expert", None),) * 4
    return jax.shard_map(
        per_device, mesh=mesh, in_specs=in_specs, out_specs=out_specs, check_vma=False
    )
```

time: 930 us -> 298 us (0.32); the launches traced: 920 us -> 298 us
  waiting for transfers between devices: 597 us -> 0 us
  Pallas kernels: 0 us -> 287 us
  local copies, waits for them, and re-layouts: 124 us -> 8.18 us
  starting transfers between devices: 111 us -> 0 us
  matrix products: 49.4 us -> 0 us
  other arithmetic: 37.1 us -> 1.83 us
    all_to_all x8 -> x0, waiting for transfers between devices: 596 us -> none  [the longest x4 328 us: send_back(): lax.all_to_all(term, 'expert', split_axis=0, concat_axis=0, tiled=True)]
    pallas_call x0 -> x1, Pallas kernels: none -> 287 us  [layers(): pl.pallas_call(kernel, out_shape=jax.ShapeDtypeStruct((4, TOK, D), BF16),...]
    all_to_all x8 -> x0, starting transfers between devices: 98.3 us -> none  [the longest x4 55.6 us: send_back(): lax.all_to_all(term, 'expert', split_axis=0, concat_axis=0, tiled=True)]
    reshape x12 -> x2, local copies, waits for them, and re-layouts: 72.4 us -> 0.08 us  [the longest x1 0.07 us: route_data(): by_col = both.transpose(1, 0, 2).reshape(TOK, micro * 4)]
    dot_general x20 -> x0, matrix products: 49.4 us -> none  [the longest x4 19.8 us: expert_part(): lax.dot_general(rows, down_w, (((1,), (1,)), ((), ())), preferred_element...]
    reduce_sum x8 -> x1, other arithmetic: 27.1 us -> 0.22 us  [route_data(): ranking = jnp.sum((jnp.cumsum(onehot, axis=1) - 1) * onehot, axis=2)]
    broadcast_in_dim x8 -> x0, local copies, waits for them, and re-layouts: 20 us -> none  [route_layout(): jnp.broadcast_to(packed[:, None], (EXPERTS, slices, CAP, width))]
    mul x12 -> x0, local copies, waits for them, and re-layouts: 18.4 us -> none  [route_layout(): grads.astype(jnp.float32)[:, None, :] * probs[:, :, None]]
  transfers between devices with their start and end apart: 10 -> 0, of which waited for: 9 -> 0; matrix products, arithmetic and copies ran while one was open for 18% -> 0% of each run, Pallas kernels for 0% -> 0%
where the time goes in v1:
time: 298 us
  Pallas kernels  287 us (96%)
  local copies, waits for them, and re-layouts  8.18 us (3%)
    pallas_call x1, Pallas kernels, layers(): pl.pallas_call(kernel, out_shape=jax.ShapeDtypeStruct((4, TOK, D), BF16),...  287 us

profile of v1, /device:TPU:0, one launch (start us, length us, event | category | flops | bytes accessed | tf_op | source)
XLA Modules:
  0.0 297.7 jit_solution(11883046957014399769)
XLA Ops:
  0.6 0.8 copy.34
  1.4 0.1 copy.36
  1.5 0.1 fusion
  1.6 0.1 reduce_window_sum.11
  1.7 0.2 select_reduce_fusion
  2.0 0.1 copy.37
  2.1 0.1 copy.38
  2.2 0.7 fusion.2
  2.9 0.1 copy.39
  3.0 0.1 tile.10
  3.1 0.6 select_maximum_fusion.meta_ref
  3.7 4.3 %reshape_squeeze.4.saved_ref = bf16[4,320,512]{2,1,0:T(8,128)(2,1)} reshape(bf16[1,4,320,2,256]{4,3,2,1,0:T(2,128)(2,1)} %param.28) | data formatting | bytes 2621440 | tf_op jit(solution)/shard_map/reshape;squeeze | solution.py:554
  8.0 287.0 %relay_layers.1 = bf16[4,32,7168]{2,1,0:T(8,128)(2,1)} custom-call(bf16[32,7168]{1,0:T(8,128)(2,1)} %bitcast.26, bf16[32,7168]{1,0:T(8,128)(2,1)} %bitcast.27, bf16[32,7168]{1,0:T(8,128)(2,1)} %na_ref.1, bf16[32,7168]{1,0:T(8,128)(2,1)} %nb_ref.1, f32[64,128]{1,0:T(8,128)} %select_maximum_fusion.meta_ref, bf16[4,320,512]{2,1,0:T(8,128)(2,1)} %reshape_squeeze.4.saved_ref, ...), custom_call_target="tpu_custom_call" | custom-call | flops 14092861440 | bytes 16777216 | tf_op jit(solution)/shard_map/relay_layers/pallas_call | solution.py:522
  295.0 2.7 fusion.3
  (3 shorter events, 0.0 us)

commit v2 on v1

--- a/solution.py
+++ b/solution.py
@@ -17,13 +17,17 @@
 NX, NY, NZ = 2, 4, 4
 ROWS = NX * NY * NZ * CAP
 BLK = ROWS // 4
-PADY = 32
+RUN = NX * CAP
 NCH = 7
 CW = D // NCH
 C1 = 640
 C3 = CW - C1
+KG = C1 // 128
+PADY = -(-KG * RUN // 16) * 16
 HA = 48
-RING = 3
+GAP = 2
+RING = GAP + 1
+DEEP = 2 * GAP + 1
 SLOTS_PHASE = 4 * NCH
 UNITS = 2 * SLOTS_PHASE
 MESH = pl.DeviceIdType.MESH
@@ -45,15 +49,19 @@
     row = lambda o: ((o[:, 0] * NY + o[:, 1]) * NZ + o[:, 2]) * CAP + o[:, 3]
     row1, row3 = row(order1), row(order3)
     from3 = (row1[:, None] == row3[None, :]).astype(np.float32)
-    from_saved = (row1[:, None] == np.arange(ROWS)[None, :]).astype(np.float32)
+    from_saved = np.concatenate(
+        [(2 * row1 + i)[:, None] == np.arange(2 * ROWS)[None, :] for i in range(2)], axis=0
+    )
     want3 = (order3[:, 0] * NZ + order3[:, 2]) * 128 + order3[:, 1] * CAP + order3[:, 3]
     want1 = np.full((NY * PADY,), -(1 << 20))
-    pick = np.zeros((BLK, NY * PADY), np.float32)
+    pick = np.zeros((KG * BLK, NY * PADY), np.float32)
     for y in range(NY):
-        for x in range(NX):
-            for k in c:
-                want1[y * PADY + x * CAP + k] = x * 128 + y * CAP + k
-                pick[(y * NX + x) * CAP + k, y * PADY + x * CAP + k] = 1
+        for group in range(KG):
+            for r in range(RUN):
+                i = y * PADY + group * RUN + r
+                want1[i] = group * 1024 + (r // CAP) * 128 + y * CAP + r % CAP
+                pick[group * BLK + y * RUN + r, i] = 1
+    off1 = np.array([k * 1024 + x * 128 for x in range(NX) for k in range(KG) for t in range(TOK)])
     lane = np.zeros((1, 128), np.float32)
     lane[0] = np.arange(128) // TOK
     off3 = (np.arange(NX * NZ * TOK) // TOK) * 128
@@ -71,6 +79,8 @@
         f(want1)[None, :],
         f(off3)[:, None],
         f(off3)[None, :],
+        f(off1)[:, None],
+        f(off1)[None, :],
         lane,
     )
 
@@ -86,12 +96,12 @@
 def kernel(
     xa_ref, xb_ref, na_ref, nb_ref, meta_ref, saved_ref, wg_ref, wu_ref, wdn_ref,
     from3_ref, to3_ref, froms_ref, pick_ref, spread_ref,
-    w3c_ref, w3r_ref, w1c_ref, w1r_ref, o3c_ref, o3r_ref, lane_ref,
+    w3c_ref, w3r_ref, w1c_ref, w1r_ref, o3c_ref, o3r_ref, o1c_ref, o1r_ref, lane_ref,
     out_ref,
-    xin, wgu, wd, svd, mr, a1, a1t, pr1, a3, a3t, pr3, fg, fu, acc1, acc3, gu1, gu3,
+    xin, ob, wgu, wd, svd, mr, mt, a1, a1t, pr1, a3, a3t, pr3, fg, fu, acc1, acc3, gu1, gu3,
     t1, y1, z1, t3, y3, y1s, y3s,
     q1, s1, r1a, r1b, y1rs, y1rr, tb1, x1r, q3, y3r, tb3, x3r, v3, s3, r3a, r3b,
-    ss, rs, mss, mrs, ls,
+    ss, rs, mss, mrs, ls, os,
 ):
     me = lax.axis_index("expert")
     pp = lax.axis_index("pipe")
@@ -185,29 +195,27 @@
         def rowpart(s):
             return mr[s, pl.ds(pl.multiple_of(m * 8, 8), 8), :]
 
-        def colpart(s):
-            return mr[s, 32:64, :]
-
         def lanes(parts):
             r = parts[-1]
             for i in range(len(parts) - 2, -1, -1):
                 r = jnp.where(lane == float(i), parts[i], r)
             return r
 
-        lane_no = lax.broadcasted_iota(jnp.int32, (1, 128), 1)
+        lane_no = lax.broadcasted_iota(jnp.int32, (1, TOK), 1)
 
         def column(arr, k):
-            return jnp.sum(jnp.where(lane_no == m * 4 + k, arr, 0.0), axis=1, keepdims=True)
+            return jnp.sum(jnp.where(lane_no == m * 8 + k, arr, 0.0), axis=1, keepdims=True)
 
         mine = (x * 40).astype(F32)
-        r1 = lanes([rowpart(z), rowpart(NZ + z)])[:, :NX * TOK]
-        o1 = o3r_ref[:, :NX * TOK]
+        near, far = rowpart(z), rowpart(NZ + z)
+        r1 = jnp.concatenate([near, jnp.where(lane == 0.0, near, far), far], axis=1)[:, :NX * KG * TOK]
+        o1 = o1r_ref[...]
         w1 = w1c_ref[...] + mine
         h0, h1 = w1 == r1[0:1] + o1, w1 == r1[1:2] + o1
         a1[st] = jnp.where(h0 | h1, 1.0, 0.0).astype(BF16)
         pr1[st] = jnp.sum(jnp.where(h0, r1[2:3], 0.0) + jnp.where(h1, r1[3:4], 0.0), axis=1, keepdims=True)
-        c1 = jnp.concatenate([colpart(z), colpart(NZ + z)], axis=0)
-        o1c = o3c_ref[:NX * TOK, :]
+        c1 = jnp.concatenate([mt[z]] * KG + [mt[NZ + z]] * KG, axis=0)
+        o1c = o1c_ref[...]
         w1t = w1r_ref[...] + mine
         a1t[st] = jnp.where(
             (column(c1, 0) + o1c == w1t) | (column(c1, 1) + o1c == w1t), 1.0, 0.0
@@ -218,7 +226,7 @@
         h0, h1 = w3 == r3[0:1] + o3, w3 == r3[1:2] + o3
         a3[st] = jnp.where(h0 | h1, 1.0, 0.0).astype(BF16)
         pr3[st] = jnp.sum(jnp.where(h0, r3[2:3], 0.0) + jnp.where(h1, r3[3:4], 0.0), axis=1, keepdims=True)
-        c3 = mr[:, 32:64, :].reshape(NX * NZ * TOK, 128)
+        c3 = mt[...].reshape(NX * NZ * TOK, TOK)
         o3t = o3c_ref[...]
         w3t = w3r_ref[...] + mine
         a3t[st] = jnp.where(
@@ -227,7 +235,7 @@
 
     def factors(st, m):
         gu = dot(froms_ref[...], svd[m])
-        gate, up = gu[:, :HD], gu[:, HD:]
+        gate, up = gu[:ROWS], gu[ROWS:]
         sig = jax.nn.sigmoid(gate)
         fg[st] = up * sig * (1.0 + gate * (1.0 - sig))
         fu[st] = gate * sig
@@ -250,7 +258,8 @@
             landing = xin.at[m, :, col(c, 0, CW)]
             rcopy(landing, landing, PIPE + st, g, c, {"pipe": pp}).wait_recv()
 
-        t1[st, c, x] = xin[m, :, col(c, 0, C1)]
+        for k in range(KG):
+            t1[st, c, x, k] = xin[m, :, col(c, 128 * k, 128)]
         rcopy(t1.at[st, c, x], t1.at[st, c, x], X1, g, c, dev(xn, y, z)).start()
         t3[st, c, x, z] = xin[m, :, col(c, C1, C3)]
         mine = t3.at[st, c, x, z]
@@ -266,14 +275,16 @@
                     d = meta_copy(k, dx, dz, landing)
                     d.wait_send()
                     d.wait_recv()
+                for i in range(NX * NZ):
+                    mt[i] = mr[i].T[:TOK]
 
             routes(st, m)
 
     def d1(p, st, c, g):
         finish(t1.at[st, c, x], t1.at[st, c, xn], X1, g, c, dev(xn, y, z))
-        rows = dot(a1[st], t1[st, c].reshape(NX * TOK, C1)) * pr1[st]
+        rows = dot(a1[st], t1[st, c].reshape(NX * KG * TOK, 128)) * pr1[st]
         ring = g % RING
-        y1s[ring] = rows.astype(BF16).reshape(NY, PADY, C1)
+        y1s[ring] = rows.astype(BF16).reshape(NY, PADY, 128)
         to_y(lambda yd: y1s.at[ring, yd], y1, st, c, g, Y1)
         y1[st, c, y] = y1s[ring, y]
         mine = t3.at[st, c, x, z]
@@ -286,7 +297,9 @@
     def d2(p, st, c, g):
         ring = g % RING
         from_y(lambda yd: y1s.at[ring, yd], y1, st, c, g, Y1)
-        z1[st, c, z] = dot(pick_ref[...], y1[st, c].reshape(NY * PADY, C1)).astype(BF16)
+        rows = dot(pick_ref[...], y1[st, c].reshape(NY * PADY, 128)).astype(BF16)
+        for k in range(KG):
+            z1[st, c, z, :, 128 * k:128 * (k + 1)] = rows[k * BLK:(k + 1) * BLK]
         mine = z1.at[st, c, z]
         rcopy(mine, mine, Z1A, g, c, dev(x, y, za)).start()
         rcopy(mine, mine, Z1A + 1, g, c, dev(x, y, zb)).start()
@@ -350,7 +363,7 @@
             gu3[st] = dot(to3_ref[...], gu1[st]).astype(BF16)
 
     def r0(p, st, c, g):
-        ring = g % RING
+        ring, deep = g % RING, g % DEEP
 
         @pl.when(g == 2 * NCH)
         def _():
@@ -358,23 +371,23 @@
             load(wu_ref, wgu.at[:, HD:2 * HD], 7).wait()
 
         part1 = dot_t(gu1[st], wgu[pl.ds(pl.multiple_of(c * CW, 128), C1), :])
-        q1[ring] = part1.astype(BF16).reshape(NZ, BLK, C1)
-        rcopy(q1.at[ring, z2, 0:HA], r1a.at[st, c, 0:HA], R1A, g, c, dev(x, y, za)).start()
-        rcopy(q1.at[ring, z2, HA:BLK], r1a.at[st, c, HA:BLK], R1A + 1, g, c, dev(x, y, zb)).start()
+        q1[deep] = part1.astype(BF16).reshape(NZ, BLK, C1)
+        rcopy(q1.at[deep, z2, 0:HA], r1a.at[st, c, 0:HA], R1A, g, c, dev(x, y, za)).start()
+        rcopy(q1.at[deep, z2, HA:BLK], r1a.at[st, c, HA:BLK], R1A + 1, g, c, dev(x, y, zb)).start()
         part3 = dot_t(gu3[st], wgu[pl.ds(pl.multiple_of(c * CW + C1, 128), C3), :])
         q3[ring] = part3.astype(BF16).reshape(NY, BLK, C3)
         to_y(lambda yd: q3.at[ring, yd], y3r, st, c, g, Y3R)
         y3r[st, c, y] = q3[ring, y]
 
     def r1(p, st, c, g):
-        ring = g % RING
-        finish(q1.at[ring, z2, 0:HA], r1a.at[st, c, 0:HA], R1A, g, c, dev(x, y, za))
-        finish(q1.at[ring, z2, HA:BLK], r1a.at[st, c, HA:BLK], R1A + 1, g, c, dev(x, y, zb))
-        s1[ring, 0, 0:HA] = (q1[ring, za, 0:HA].astype(F32) + r1a[st, c, 0:HA].astype(F32)).astype(BF16)
-        s1[ring, 0, HA:BLK] = q1[ring, za, HA:BLK]
+        ring, deep = g % RING, g % DEEP
+        finish(q1.at[deep, z2, 0:HA], r1a.at[st, c, 0:HA], R1A, g, c, dev(x, y, za))
+        finish(q1.at[deep, z2, HA:BLK], r1a.at[st, c, HA:BLK], R1A + 1, g, c, dev(x, y, zb))
+        s1[ring, 0, 0:HA] = (q1[deep, za, 0:HA].astype(F32) + r1a[st, c, 0:HA].astype(F32)).astype(BF16)
+        s1[ring, 0, HA:BLK] = q1[deep, za, HA:BLK]
         rcopy(s1.at[ring, 0], r1b.at[st, c, 0], R1B, g, c, dev(x, y, za)).start()
-        s1[ring, 1, 0:HA] = q1[ring, zb, 0:HA]
-        s1[ring, 1, HA:BLK] = (q1[ring, zb, HA:BLK].astype(F32) + r1a[st, c, HA:BLK].astype(F32)).astype(BF16)
+        s1[ring, 1, 0:HA] = q1[deep, zb, 0:HA]
+        s1[ring, 1, HA:BLK] = (q1[deep, zb, HA:BLK].astype(F32) + r1a[st, c, HA:BLK].astype(F32)).astype(BF16)
         rcopy(s1.at[ring, 1], r1b.at[st, c, 1], R1B + 1, g, c, dev(x, y, zb)).start()
         from_y(lambda yd: q3.at[ring, yd], y3r, st, c, g, Y3R)
         sums = dot(a3t[st], y3r[st, c].reshape(ROWS, C3))
@@ -382,52 +395,61 @@
         rcopy(tb3.at[ring, xn], x3r.at[st, c], X3R, g, c, dev(xn, y, z)).start()
 
     def r2(p, st, c, g):
-        ring = g % RING
+        ring, deep = g % RING, g % DEEP
         finish(s1.at[ring, 0], r1b.at[st, c, 0], R1B, g, c, dev(x, y, za))
         finish(s1.at[ring, 1], r1b.at[st, c, 1], R1B + 1, g, c, dev(x, y, zb))
-        total = q1[ring, z].astype(F32) + r1b[st, c, 0].astype(F32) + r1b[st, c, 1].astype(F32)
-        rows = dot(spread_ref[...], total.astype(BF16))
-        y1rs[ring] = rows.astype(BF16).reshape(NY, PADY, C1)
+        total = q1[deep, z].astype(F32) + r1b[st, c, 0].astype(F32) + r1b[st, c, 1].astype(F32)
+        total = total.astype(BF16)
+        groups = jnp.concatenate([total[:, 128 * k:128 * (k + 1)] for k in range(KG)], axis=0)
+        rows = dot(spread_ref[...], groups)
+        y1rs[ring] = rows.astype(BF16).reshape(NY, PADY, 128)
         to_y(lambda yd: y1rs.at[ring, yd], y1rr, st, c, g, Y1R)
         y1rr[st, c, y] = y1rs[ring, y]
         finish(tb3.at[ring, xn], x3r.at[st, c], X3R, g, c, dev(xn, y, z))
         v = tb3[ring, x].astype(F32) + x3r[st, c].astype(F32)
-        v3[ring] = v.astype(BF16).reshape(NZ, TOK, C3)
-        rcopy(v3.at[ring, z2, 0:16], r3a.at[st, c, 0:16], R3A, g, c, dev(x, y, za)).start()
-        rcopy(v3.at[ring, z2, 16:32], r3a.at[st, c, 16:32], R3A + 1, g, c, dev(x, y, zb)).start()
+        v3[deep] = v.astype(BF16).reshape(NZ, TOK, C3)
+        rcopy(v3.at[deep, z2, 0:16], r3a.at[st, c, 0:16], R3A, g, c, dev(x, y, za)).start()
+        rcopy(v3.at[deep, z2, 16:32], r3a.at[st, c, 16:32], R3A + 1, g, c, dev(x, y, zb)).start()
 
     def r3(p, st, c, g):
-        ring = g % RING
+        ring, deep = g % RING, g % DEEP
         from_y(lambda yd: y1rs.at[ring, yd], y1rr, st, c, g, Y1R)
-        sums = dot(a1t[st], y1rr[st, c].reshape(NY * PADY, C1))
-        tb1[ring] = sums.astype(BF16).reshape(NX, TOK, C1)
+        sums = dot(a1t[st], y1rr[st, c].reshape(NY * PADY, 128))
+        tb1[ring] = sums.astype(BF16).reshape(NX, KG, TOK, 128)
         rcopy(tb1.at[ring, xn], x1r.at[st, c], X1R, g, c, dev(xn, y, z)).start()
-        finish(v3.at[ring, z2, 0:16], r3a.at[st, c, 0:16], R3A, g, c, dev(x, y, za))
-        finish(v3.at[ring, z2, 16:32], r3a.at[st, c, 16:32], R3A + 1, g, c, dev(x, y, zb))
-        s3[ring, 0, 0:16] = (v3[ring, za, 0:16].astype(F32) + r3a[st, c, 0:16].astype(F32)).astype(BF16)
-        s3[ring, 0, 16:32] = v3[ring, za, 16:32]
+        finish(v3.at[deep, z2, 0:16], r3a.at[st, c, 0:16], R3A, g, c, dev(x, y, za))
+        finish(v3.at[deep, z2, 16:32], r3a.at[st, c, 16:32], R3A + 1, g, c, dev(x, y, zb))
+        s3[ring, 0, 0:16] = (v3[deep, za, 0:16].astype(F32) + r3a[st, c, 0:16].astype(F32)).astype(BF16)
+        s3[ring, 0, 16:32] = v3[deep, za, 16:32]
         rcopy(s3.at[ring, 0], r3b.at[st, c, 0], R3B, g, c, dev(x, y, za)).start()
-        s3[ring, 1, 0:16] = v3[ring, zb, 0:16]
-        s3[ring, 1, 16:32] = (v3[ring, zb, 16:32].astype(F32) + r3a[st, c, 16:32].astype(F32)).astype(BF16)
+        s3[ring, 1, 0:16] = v3[deep, zb, 0:16]
+        s3[ring, 1, 16:32] = (v3[deep, zb, 16:32].astype(F32) + r3a[st, c, 16:32].astype(F32)).astype(BF16)
         rcopy(s3.at[ring, 1], r3b.at[st, c, 1], R3B + 1, g, c, dev(x, y, zb)).start()
+
+    def out_copy(m, c, ring):
+        cols = col(c, 0, CW)
+        return pltpu.make_async_copy(ob.at[m, :, cols], out_ref.at[m, :, cols], os.at[ring])
 
     def pipe_copy(m, st, c, g, to):
         cols = col(c, 0, CW)
-        return rcopy(out_ref.at[m, :, cols], xin.at[m + 2, :, cols], PIPE + st, g, c, {"pipe": to})
+        return rcopy(ob.at[m, :, cols], xin.at[m + 2, :, cols], PIPE + st, g, c, {"pipe": to})
 
     def r4(p, st, c, g):
-        ring = g % RING
+        ring, deep = g % RING, g % DEEP
         m = 2 * p + st
         finish(tb1.at[ring, xn], x1r.at[st, c], X1R, g, c, dev(xn, y, z))
         finish(s3.at[ring, 0], r3b.at[st, c, 0], R3B, g, c, dev(x, y, za))
         finish(s3.at[ring, 1], r3b.at[st, c, 1], R3B + 1, g, c, dev(x, y, zb))
-        cols1, cols3 = col(c, 0, C1), col(c, C1, C3)
-        o1 = xin[m, :, cols1].astype(F32) + (tb1[ring, x].astype(F32) + x1r[st, c].astype(F32))
-        out_ref[m, :, cols1] = o1.astype(BF16)
+        for k in range(KG):
+            cols = col(c, 128 * k, 128)
+            o1 = xin[m, :, cols].astype(F32) + (tb1[ring, x, k].astype(F32) + x1r[st, c, k].astype(F32))
+            ob[m, :, cols] = o1.astype(BF16)
+        cols3 = col(c, C1, C3)
         o3 = xin[m, :, cols3].astype(F32) + (
-            v3[ring, z].astype(F32) + r3b[st, c, 0].astype(F32) + r3b[st, c, 1].astype(F32)
+            v3[deep, z].astype(F32) + r3b[st, c, 0].astype(F32) + r3b[st, c, 1].astype(F32)
         )
-        out_ref[m, :, cols3] = o3.astype(BF16)
+        ob[m, :, cols3] = o3.astype(BF16)
+        out_copy(m, c, ring).start()
 
         @pl.when((p == 0) & (st == 0) & (pp > 0))
         def _():
@@ -438,6 +460,8 @@
             pipe_copy(1, 1, c, g, pp + 1).start()
 
     def r5(p, st, c, g):
+        out_copy(2 * p + st, c, g % RING).wait()
+
         @pl.when((p == 0) & (st == 0) & (pp > 0))
         def _():
             pipe_copy(0, 0, c, g, pp - 1).wait_send()
@@ -458,12 +482,12 @@
 
     def tick(t, carry):
         for k, body in enumerate([d0, d1, d2, d3, d4]):
-            stage(t, k, False, body)
+            stage(t, GAP * k, False, body)
         for k, body in enumerate([r0, r1, r2, r3, r4, r5]):
-            stage(t, k, True, body)
+            stage(t, GAP * k, True, body)
         return carry
 
-    lax.fori_loop(0, UNITS + 5, tick, 0)
+    lax.fori_loop(0, UNITS + 5 * GAP, tick, 0)
 
 
 def layers(xa, xb, na, nb, meta, saved, wg, wu, wdn):
@@ -473,12 +497,14 @@
     V = pltpu.VMEM
     scratch = [
         V((4, TOK, D), BF16),
+        V((4, TOK, D), BF16),
         V((D, 2 * HD), BF16),
         V((HD, D), BF16),
-        V((4, ROWS, 2 * HD), BF16),
-        V((NX * NZ, 64, 128), F32),
-        V((2, NY * PADY, NX * TOK), BF16),
-        V((2, NX * TOK, NY * PADY), BF16),
+        V((4, 2 * ROWS, HD), BF16),
+        V((NX * NZ, 32, 128), F32),
+        V((NX * NZ, TOK, TOK), F32),
+        V((2, NY * PADY, NX * KG * TOK), BF16),
+        V((2, NX * KG * TOK, NY * PADY), BF16),
         V((2, NY * PADY, 1), F32),
         V((2, ROWS, NX * NZ * TOK), BF16),
         V((2, NX * NZ * TOK, ROWS), BF16),
@@ -489,26 +515,26 @@
         V((2, ROWS, HD), F32),
         V((2, ROWS, 2 * HD), BF16),
         V((2, ROWS, 2 * HD), BF16),
-        V((2, NCH, NX, TOK, C1), BF16),
-        V((2, NCH, NY, PADY, C1), BF16),
+        V((2, NCH, NX, KG, TOK, 128), BF16),
+        V((2, NCH, NY, PADY, 128), BF16),
         V((2, NCH, NZ, BLK, C1), BF16),
         V((2, NCH, NX, NZ, TOK, C3), BF16),
         V((2, NCH, NY, BLK, C3), BF16),
-        V((RING, NY, PADY, C1), BF16),
+        V((RING, NY, PADY, 128), BF16),
         V((RING, NY, BLK, C3), BF16),
-        V((RING, NZ, BLK, C1), BF16),
+        V((DEEP, NZ, BLK, C1), BF16),
         V((RING, 2, BLK, C1), BF16),
         V((2, NCH, BLK, C1), BF16),
         V((2, NCH, 2, BLK, C1), BF16),
-        V((RING, NY, PADY, C1), BF16),
-        V((2, NCH, NY, PADY, C1), BF16),
-        V((RING, NX, TOK, C1), BF16),
-        V((2, NCH, TOK, C1), BF16),
+        V((RING, NY, PADY, 128), BF16),
+        V((2, NCH, NY, PADY, 128), BF16),
+        V((RING, NX, KG, TOK, 128), BF16),
+        V((2, NCH, KG, TOK, 128), BF16),
         V((RING, NY, BLK, C3), BF16),
         V((2, NCH, NY, BLK, C3), BF16),
         V((RING, NX, NZ * TOK, C3), BF16),
         V((2, NCH, NZ * TOK, C3), BF16),
-        V((RING, NZ, TOK, C3), BF16),
+        V((DEEP, NZ, TOK, C3), BF16),
         V((RING, 2, TOK, C3), BF16),
         V((2, NCH, TOK, C3), BF16),
         V((2, NCH, 2, TOK, C3), BF16),
@@ -517,13 +543,14 @@
         pltpu.SemaphoreType.DMA((8,)),
         pltpu.SemaphoreType.DMA((8,)),
         pltpu.SemaphoreType.DMA((8,)),
+        pltpu.SemaphoreType.DMA((RING,)),
     ]
     flops = 4 * 2 * ROWS * D * HD * 3
     return pl.pallas_call(
         kernel,
         out_shape=jax.ShapeDtypeStruct((4, TOK, D), BF16),
         in_specs=[any_spec] * 4 + [vmem] + [any_spec] * 4 + [vmem] * len(consts),
-        out_specs=vmem,
+        out_specs=any_spec,
         scratch_shapes=scratch,
         compiler_params=pltpu.CompilerParams(
             collective_id=0, has_side_effects=True, vmem_limit_bytes=63 * 2**20
@@ -536,22 +563,20 @@
 def route_data(ids, probs):
     micro = ids.shape[0]
     flat = ids.reshape(micro, TOK * TOPK)
-    onehot = (flat[:, :, None] == jnp.arange(EXPERTS, dtype=jnp.int32)).astype(jnp.int32)
-    ranking = jnp.sum((jnp.cumsum(onehot, axis=1) - 1) * onehot, axis=2)
+    pair = jnp.arange(TOK * TOPK)
+    earlier = (flat[:, :, None] == flat[:, None, :]) & (pair[None, :] < pair[:, None])
+    ranking = jnp.sum(earlier.astype(jnp.int32), axis=2)
     slots = (flat * CAP + ranking).reshape(micro, TOK, TOPK).astype(F32)
     both = jnp.concatenate([slots, probs], axis=2)
-    by_row = jnp.tile(both.transpose(0, 2, 1), (1, 1, 128 // TOK))
-    by_row = jnp.pad(by_row, ((0, 0), (0, 4), (0, 0))).reshape(micro * 8, 128)
-    by_col = both.transpose(1, 0, 2).reshape(TOK, micro * 4)
-    by_col = jnp.pad(by_col, ((0, 0), (0, 128 - micro * 4)))
-    return jnp.concatenate([by_row, by_col], axis=0)
+    by_row = jnp.tile(both.transpose(0, 2, 1), (1, 2, 128 // TOK))
+    return by_row.reshape(micro * 8, 128)
 
 
 def per_device(
     held_a, held_b, new_a, new_b, expert_ids, route_probs, saved_gate_up, w_gate, w_up, w_down
 ):
     meta = route_data(expert_ids[0], route_probs[0])
-    saved = saved_gate_up[0].reshape(4, ROWS, 2 * HD)
+    saved = saved_gate_up[0].reshape(4, 2 * ROWS, HD)
     out = layers(
         held_a[0], held_b[0], new_a, new_b, meta, saved, w_gate[0], w_up[0], w_down[0]
     )

time: 298 us -> 265 us (0.89)
  Pallas kernels: 287 us -> 255 us
    pallas_call x1, Pallas kernels: 287 us -> 255 us  [layers(): pl.pallas_call(kernel, out_shape=jax.ShapeDtypeStruct((4, TOK, D), BF16),...]
where the time goes in v2:
time: 265 us
  Pallas kernels  255 us (96%)
  local copies, waits for them, and re-layouts  8.54 us (3%)
    pallas_call x1, Pallas kernels, layers(): pl.pallas_call(kernel, out_shape=jax.ShapeDtypeStruct((4, TOK, D), BF16),...  255 us

profile of v2, /device:TPU:0, one launch (start us, length us, event | category | flops | bytes accessed | tf_op | source)
XLA Modules:
  0.0 265.1 jit_solution(12807700774172631798)
XLA Ops:
  0.6 0.8 copy.39
  1.4 0.1 copy.41
  1.5 0.2 convert_reduce_fusion
  1.7 0.1 copy.43
  1.9 0.1 copy.44
  2.0 0.7 maximum_bitcast_fusion
  2.7 0.7 tile.9.meta_ref
  3.4 4.1 %reshape_squeeze.4.saved_ref = bf16[4,640,256]{2,1,0:T(8,128)(2,1)} reshape(bf16[1,4,320,2,256]{4,3,2,1,0:T(2,128)(2,1)} %param.30) | data formatting | bytes 2621440 | tf_op jit(solution)/shard_map/reshape;squeeze | solution.py:579
  7.5 254.9 %relay_layers.1 = bf16[4,32,7168]{2,1,0:T(8,128)(2,1)} custom-call(bf16[32,7168]{1,0:T(8,128)(2,1)} %bitcast.20, bf16[32,7168]{1,0:T(8,128)(2,1)} %bitcast.21, bf16[32,7168]{1,0:T(8,128)(2,1)} %na_ref.1, bf16[32,7168]{1,0:T(8,128)(2,1)} %nb_ref.1, f32[32,128]{1,0:T(8,128)} %tile.9.meta_ref, bf16[4,640,256]{2,1,0:T(8,128)(2,1)} %reshape_squeeze.4.saved_ref, ...), custom_call_target="tpu_custom_call" | custom-call | flops 14092861440 | bytes 16777216 | tf_op jit(solution)/shard_map/relay_layers/pallas_call | solution.py:549
  262.4 2.7 %fusion.1 = (bf16[1,32,7168]{2,1,0:T(8,128)(2,1)}, bf16[1,32,7168]{2,1,0:T(8,128)(2,1)}, bf16[1,32,7168]{2,1,0:T(8,128)(2,1)}, bf16[1,32,7168]{2,1,0:T(8,128)(2,1)}) fusion(bf16[4,32,7168]{2,1,0:T(8,128)(2,1)} %relay_layers.1), kind=kLoop, calls=%fused_computation.5 | loop fusion | bytes 3670016 | tf_op jit(solution)/shard_map/slice | solution.py:583
  (3 shorter events, 0.1 us)

commit v3 on v2

--- a/solution.py
+++ b/solution.py
@@ -25,7 +25,14 @@
 KG = C1 // 128
 PADY = -(-KG * RUN // 16) * 16
 HA = 48
+S1 = 512
+S3 = CW - S1
+KD = S1 // 128
+PADD = -(-KD * RUN // 16) * 16
+H1, H3 = S1 // 2, S3 // 2
 GAP = 2
+DISPATCH = (0, 2, 4, 6, 8, 10)
+RETURN = (2, 4, 6, 8, 10, 12)
 RING = GAP + 1
 DEEP = 2 * GAP + 1
 SLOTS_PHASE = 4 * NCH
@@ -53,15 +60,21 @@
         [(2 * row1 + i)[:, None] == np.arange(2 * ROWS)[None, :] for i in range(2)], axis=0
     )
     want3 = (order3[:, 0] * NZ + order3[:, 2]) * 128 + order3[:, 1] * CAP + order3[:, 3]
-    want1 = np.full((NY * PADY,), -(1 << 20))
-    pick = np.zeros((KG * BLK, NY * PADY), np.float32)
-    for y in range(NY):
-        for group in range(KG):
-            for r in range(RUN):
-                i = y * PADY + group * RUN + r
-                want1[i] = group * 1024 + (r // CAP) * 128 + y * CAP + r % CAP
-                pick[group * BLK + y * RUN + r, i] = 1
-    off1 = np.array([k * 1024 + x * 128 for x in range(NX) for k in range(KG) for t in range(TOK)])
+
+    def stacked(groups, pad):
+        want = np.full((NY * pad,), -(1 << 20))
+        pick = np.zeros((groups * BLK, NY * pad), np.float32)
+        for y in range(NY):
+            for group in range(groups):
+                for r in range(RUN):
+                    i = y * pad + group * RUN + r
+                    want[i] = group * 1024 + (r // CAP) * 128 + y * CAP + r % CAP
+                    pick[group * BLK + y * RUN + r, i] = 1
+        off = [k * 1024 + x * 128 for x in range(NX) for k in range(groups) for t in range(TOK)]
+        return want, pick, np.array(off)
+
+    want1, pick1, off1 = stacked(KD, PADD)
+    want1r, pick1r, off1r = stacked(KG, PADY)
     lane = np.zeros((1, 128), np.float32)
     lane[0] = np.arange(128) // TOK
     off3 = (np.arange(NX * NZ * TOK) // TOK) * 128
@@ -71,15 +84,15 @@
         b(from3),
         b(from3.T),
         b(from_saved),
-        b(pick),
-        b(pick.T),
+        b(pick1),
+        b(pick1r.T),
         f(want3)[:, None],
         f(want3)[None, :],
         f(want1)[:, None],
-        f(want1)[None, :],
+        f(want1r)[None, :],
         f(off3)[:, None],
         f(off3)[None, :],
-        f(off1)[:, None],
+        f(off1r)[:, None],
         f(off1)[None, :],
         lane,
     )
@@ -98,10 +111,10 @@
     from3_ref, to3_ref, froms_ref, pick_ref, spread_ref,
     w3c_ref, w3r_ref, w1c_ref, w1r_ref, o3c_ref, o3r_ref, o1c_ref, o1r_ref, lane_ref,
     out_ref,
-    xin, ob, wgu, wd, svd, mr, mt, a1, a1t, pr1, a3, a3t, pr3, fg, fu, acc1, acc3, gu1, gu3,
-    t1, y1, z1, t3, y3, y1s, y3s,
+    xin, ob, wgu, wd, svd, mr, mt, a1, a1t, pr1, a3, a3t, pr3, fg, fu, acc1, acc3, accp, gu1, gu3,
+    t1, y1, z1, t3, y3, y1s, y3s, zs, wp, hs, hr,
     q1, s1, r1a, r1b, y1rs, y1rr, tb1, x1r, q3, y3r, tb3, x3r, v3, s3, r3a, r3b,
-    ss, rs, mss, mrs, ls, os,
+    ss, rs, mss, mrs, ls, os, wss, wrs, hss, hrs,
 ):
     me = lax.axis_index("expert")
     pp = lax.axis_index("pipe")
@@ -111,6 +124,13 @@
     za = (z + 1 + 2 * core) % NZ
     zb = (z + 3 - 2 * core) % NZ
     z2 = (z + 2) % NZ
+    near1, near2 = z + 1 - 2 * (z % 2), 3 - z
+
+    def pairing(c):
+        q = c % 2
+        d = jnp.where(q == 0, near1, near2)
+        h = jnp.where(q == 0, near2, near1)
+        return q, d, h, jnp.where(q == 0, z // 2, ((z + 1) // 2) % 2)
 
     def dev(px, py, pz):
         return {"expert": (px * NY + py) * NZ + pz}
@@ -208,7 +228,7 @@
 
         mine = (x * 40).astype(F32)
         near, far = rowpart(z), rowpart(NZ + z)
-        r1 = jnp.concatenate([near, jnp.where(lane == 0.0, near, far), far], axis=1)[:, :NX * KG * TOK]
+        r1 = jnp.concatenate([near, far], axis=1)
         o1 = o1r_ref[...]
         w1 = w1c_ref[...] + mine
         h0, h1 = w1 == r1[0:1] + o1, w1 == r1[1:2] + o1
@@ -250,6 +270,27 @@
             yd, ys = (y + dy) % NY, (y - dy + NY) % NY
             finish(src_of(yd), buf.at[st, c, ys], kind + dy - 1, g, c, dev(x, yd, z))
 
+    def half_col(c, off, half, width):
+        return pl.ds(pl.multiple_of(c * CW + off + half * width, 128), width)
+
+    def weights(c, h, half, piece):
+        cols = half_col(c, piece * S1, 1 - half, H1)
+        return pltpu.make_async_remote_copy(
+            src_ref=wd.at[:, cols], dst_ref=wp.at[c, piece], send_sem=wss.at[c, piece],
+            recv_sem=wrs.at[c, piece], device_id=dev(x, y, h), device_id_type=MESH,
+        )
+
+    def partials(st, q, h):
+        return pltpu.make_async_remote_copy(
+            src_ref=hs.at[q], dst_ref=hr.at[st, q], send_sem=hss.at[q],
+            recv_sem=hrs.at[st, q], device_id=dev(x, y, h), device_id_type=MESH,
+        )
+
+    def reorder(a):
+        high = a.astype(BF16)
+        low = (a - high.astype(F32)).astype(BF16)
+        return dot(from3_ref[...], high) + dot(from3_ref[...], low)
+
     def d0(p, st, c, g):
         m = 2 * p + st
 
@@ -258,17 +299,27 @@
             landing = xin.at[m, :, col(c, 0, CW)]
             rcopy(landing, landing, PIPE + st, g, c, {"pipe": pp}).wait_recv()
 
-        for k in range(KG):
+        q, d, h, half = pairing(c)
+        for k in range(KD):
             t1[st, c, x, k] = xin[m, :, col(c, 128 * k, 128)]
         rcopy(t1.at[st, c, x], t1.at[st, c, x], X1, g, c, dev(xn, y, z)).start()
-        t3[st, c, x, z] = xin[m, :, col(c, C1, C3)]
+        t3[st, c, x, z] = xin[m, :, half_col(c, S1, half, H3)]
         mine = t3.at[st, c, x, z]
-        rcopy(mine, mine, Z3A, g, c, dev(x, y, za)).start()
-        rcopy(mine, mine, Z3A + 1, g, c, dev(x, y, zb)).start()
-
-        @pl.when(c == 0)
+        rcopy(mine, mine, Z3A + q, g, c, dev(x, y, d)).start()
+        rcopy(xin.at[m, :, half_col(c, S1, 1 - half, H3)], mine, Z3A + 1 - q, g, c, dev(x, y, h)).start()
+
+        @pl.when((p == 0) & (st == 0))
         def _():
             @pl.when(g == 0)
+            def _():
+                load(wdn_ref, wd, 5).wait()
+
+            weights(c, h, half, 0).start()
+            weights(c, h, half, 1).start()
+
+        @pl.when(c == 1)
+        def _():
+            @pl.when(g == 1)
             def _():
                 for k, (dx, dz) in enumerate(metas):
                     landing = ((x + dx) % NX) * NZ + (z - dz + NZ) % NZ
@@ -281,30 +332,32 @@
             routes(st, m)
 
     def d1(p, st, c, g):
+        q, d, h, half = pairing(c)
+        ring = g % RING
         finish(t1.at[st, c, x], t1.at[st, c, xn], X1, g, c, dev(xn, y, z))
-        rows = dot(a1[st], t1[st, c].reshape(NX * KG * TOK, 128)) * pr1[st]
-        ring = g % RING
-        y1s[ring] = rows.astype(BF16).reshape(NY, PADY, 128)
+        rows = dot(a1[st], t1[st, c].reshape(NX * KD * TOK, 128)) * pr1[st]
+        y1s[ring] = rows.astype(BF16).reshape(NY, PADD, 128)
         to_y(lambda yd: y1s.at[ring, yd], y1, st, c, g, Y1)
         y1[st, c, y] = y1s[ring, y]
         mine = t3.at[st, c, x, z]
-        finish(mine, t3.at[st, c, x, zb], Z3A, g, c, dev(x, y, za))
-        finish(mine, t3.at[st, c, x, za], Z3A + 1, g, c, dev(x, y, zb))
-        fwd_a, fwd_b = t3.at[st, c, x, zb, 0:16], t3.at[st, c, x, za, 16:32]
-        rcopy(fwd_a, fwd_a, Z3B, g, c, dev(x, y, za)).start()
-        rcopy(fwd_b, fwd_b, Z3B + 1, g, c, dev(x, y, zb)).start()
+        finish(mine, t3.at[st, c, x, d], Z3A + q, g, c, dev(x, y, d))
+        finish(xin.at[2 * p + st, :, half_col(c, S1, 1 - half, H3)], t3.at[st, c, x, h], Z3A + 1 - q, g, c, dev(x, y, h))
+        fwd = t3.at[st, c, x, h]
+        rcopy(fwd, fwd, Z3B + q, g, c, dev(x, y, d)).start()
 
     def d2(p, st, c, g):
+        q, d, h, half = pairing(c)
         ring = g % RING
         from_y(lambda yd: y1s.at[ring, yd], y1, st, c, g, Y1)
-        rows = dot(pick_ref[...], y1[st, c].reshape(NY * PADY, 128)).astype(BF16)
-        for k in range(KG):
-            z1[st, c, z, :, 128 * k:128 * (k + 1)] = rows[k * BLK:(k + 1) * BLK]
+        rows = dot(pick_ref[...], y1[st, c].reshape(NY * PADD, 128)).astype(BF16)
+        for k in range(KD):
+            lo = 128 * k % H1
+            zs[ring, 128 * k // H1, :, lo:lo + 128] = rows[k * BLK:(k + 1) * BLK]
+        z1[st, c, z] = zs[ring, half]
         mine = z1.at[st, c, z]
-        rcopy(mine, mine, Z1A, g, c, dev(x, y, za)).start()
-        rcopy(mine, mine, Z1A + 1, g, c, dev(x, y, zb)).start()
-        finish(t3.at[st, c, x, zb, 0:16], t3.at[st, c, x, z2, 0:16], Z3B, g, c, dev(x, y, za))
-        finish(t3.at[st, c, x, za, 16:32], t3.at[st, c, x, z2, 16:32], Z3B + 1, g, c, dev(x, y, zb))
+        rcopy(mine, mine, Z1A + q, g, c, dev(x, y, d)).start()
+        rcopy(zs.at[ring, 1 - half], mine, Z1A + 1 - q, g, c, dev(x, y, h)).start()
+        finish(t3.at[st, c, x, h], t3.at[st, c, x, z2], Z3B + q, g, c, dev(x, y, d))
         rcopy(t3.at[st, c, x], t3.at[st, c, x], X3, g, c, dev(xn, y, z)).start()
 
         @pl.when(c == 0)
@@ -316,50 +369,76 @@
             factors(st, 2 * p + st)
 
     def d3(p, st, c, g):
+        q, d, h, half = pairing(c)
         ring = g % RING
-        mine = z1.at[st, c, z]
-        finish(mine, z1.at[st, c, zb], Z1A, g, c, dev(x, y, za))
-        finish(mine, z1.at[st, c, za], Z1A + 1, g, c, dev(x, y, zb))
-        fwd_a, fwd_b = z1.at[st, c, zb, 0:HA], z1.at[st, c, za, HA:BLK]
-        rcopy(fwd_a, fwd_a, Z1F, g, c, dev(x, y, za)).start()
-        rcopy(fwd_b, fwd_b, Z1F + 1, g, c, dev(x, y, zb)).start()
+        finish(z1.at[st, c, z], z1.at[st, c, d], Z1A + q, g, c, dev(x, y, d))
+        finish(zs.at[ring, 1 - half], z1.at[st, c, h], Z1A + 1 - q, g, c, dev(x, y, h))
+        fwd = z1.at[st, c, h]
+        rcopy(fwd, fwd, Z1F + q, g, c, dev(x, y, d)).start()
         finish(t3.at[st, c, x], t3.at[st, c, xn], X3, g, c, dev(xn, y, z))
-        rows = dot(a3[st], t3[st, c].reshape(NX * NZ * TOK, C3)) * pr3[st]
-        y3s[ring] = rows.astype(BF16).reshape(NY, BLK, C3)
+        rows = dot(a3[st], t3[st, c].reshape(NX * NZ * TOK, H3)) * pr3[st]
+        y3s[ring] = rows.astype(BF16).reshape(NY, BLK, H3)
         to_y(lambda yd: y3s.at[ring, yd], y3, st, c, g, Y3)
         y3[st, c, y] = y3s[ring, y]
 
     def d4(p, st, c, g):
+        q, d, h, half = pairing(c)
         ring = g % RING
-        finish(z1.at[st, c, zb, 0:HA], z1.at[st, c, z2, 0:HA], Z1F, g, c, dev(x, y, za))
-        finish(z1.at[st, c, za, HA:BLK], z1.at[st, c, z2, HA:BLK], Z1F + 1, g, c, dev(x, y, zb))
+        finish(z1.at[st, c, h], z1.at[st, c, z2], Z1F + q, g, c, dev(x, y, d))
         from_y(lambda yd: y3s.at[ring, yd], y3, st, c, g, Y3)
 
-        @pl.when(g == 0)
-        def _():
-            load(wdn_ref, wd, 5).wait()
-
-        h1 = dot_t(z1[st, c].reshape(ROWS, C1), wd[:, col(c, 0, C1)])
-        h3 = dot_t(y3[st, c].reshape(ROWS, C3), wd[:, col(c, C1, C3)])
+        @pl.when((p == 0) & (st == 0))
+        def _():
+            for piece in range(2):
+                w = weights(c, h, half, piece)
+                w.wait_send()
+                w.wait_recv()
+
+        rows1, rows3 = z1[st, c].reshape(ROWS, H1), y3[st, c].reshape(ROWS, H3)
+        m1 = dot_t(rows1, wd[:, half_col(c, 0, half, H1)])
+        m3 = dot_t(rows3, wd[:, half_col(c, S1, half, H3)])
+        o1, o3 = dot_t(rows1, wp[c, 0]), dot_t(rows3, wp[c, 1])
 
         @pl.when(c == 0)
         def _():
-            acc1[st] = h1
-            acc3[st] = h3
+            acc1[st] = m1
+            acc3[st] = m3
 
         @pl.when(c > 0)
         def _():
-            acc1[st] += h1
-            acc3[st] += h3
+            acc1[st] += m1
+            acc3[st] += m3
+
+        @pl.when(c < 2)
+        def _():
+            accp[st, q, 0] = o1
+            accp[st, q, 1] = o3
+
+        @pl.when(c >= 2)
+        def _():
+            accp[st, q, 0] += o1
+            accp[st, q, 1] += o3
+
+        @pl.when(c >= NCH - 2)
+        def _():
+            hs[q] = (accp[st, q, 0] + reorder(accp[st, q, 1])).astype(BF16)
+            partials(st, q, h).start()
+
+    def d5(p, st, c, g):
+        q, d, h, half = pairing(c)
+
+        @pl.when(c >= NCH - 2)
+        def _():
+            w = partials(st, q, h)
+            w.wait_send()
+            w.wait_recv()
 
         @pl.when(c == NCH - 1)
         def _():
-            other = acc3[st]
-            high = other.astype(BF16)
-            low = (other - high.astype(F32)).astype(BF16)
-            h = acc1[st] + dot(from3_ref[...], high) + dot(from3_ref[...], low)
-            gu1[st, :, 0:HD] = (h * fg[st]).astype(BF16)
-            gu1[st, :, HD:2 * HD] = (h * fu[st]).astype(BF16)
+            both = hr[st, 0].astype(F32) + hr[st, 1].astype(F32)
+            h_all = acc1[st] + reorder(acc3[st]) + both
+            gu1[st, :, 0:HD] = (h_all * fg[st]).astype(BF16)
+            gu1[st, :, HD:2 * HD] = (h_all * fu[st]).astype(BF16)
             gu3[st] = dot(to3_ref[...], gu1[st]).astype(BF16)
 
     def r0(p, st, c, g):
@@ -481,13 +560,13 @@
             body(p, (w // NCH) % 2, w % NCH, g)
 
     def tick(t, carry):
-        for k, body in enumerate([d0, d1, d2, d3, d4]):
-            stage(t, GAP * k, False, body)
-        for k, body in enumerate([r0, r1, r2, r3, r4, r5]):
-            stage(t, GAP * k, True, body)
+        for k, body in zip(DISPATCH, [d0, d1, d2, d3, d4, d5]):
+            stage(t, k, False, body)
+        for k, body in zip(RETURN, [r0, r1, r2, r3, r4, r5]):
+            stage(t, k, True, body)
         return carry
 
-    lax.fori_loop(0, UNITS + 5 * GAP, tick, 0)
+    lax.fori_loop(0, UNITS + RETURN[-1], tick, 0)
 
 
 def layers(xa, xb, na, nb, meta, saved, wg, wu, wdn):
@@ -503,9 +582,9 @@
         V((4, 2 * ROWS, HD), BF16),
         V((NX * NZ, 32, 128), F32),
         V((NX * NZ, TOK, TOK), F32),
-        V((2, NY * PADY, NX * KG * TOK), BF16),
+        V((2, NY * PADD, NX * KD * TOK), BF16),
         V((2, NX * KG * TOK, NY * PADY), BF16),
-        V((2, NY * PADY, 1), F32),
+        V((2, NY * PADD, 1), F32),
         V((2, ROWS, NX * NZ * TOK), BF16),
         V((2, NX * NZ * TOK, ROWS), BF16),
         V((2, ROWS, 1), F32),
@@ -513,15 +592,20 @@
         V((2, ROWS, HD), F32),
         V((2, ROWS, HD), F32),
         V((2, ROWS, HD), F32),
+        V((2, 2, 2, ROWS, HD), F32),
         V((2, ROWS, 2 * HD), BF16),
         V((2, ROWS, 2 * HD), BF16),
-        V((2, NCH, NX, KG, TOK, 128), BF16),
-        V((2, NCH, NY, PADY, 128), BF16),
-        V((2, NCH, NZ, BLK, C1), BF16),
-        V((2, NCH, NX, NZ, TOK, C3), BF16),
-        V((2, NCH, NY, BLK, C3), BF16),
-        V((RING, NY, PADY, 128), BF16),
-        V((RING, NY, BLK, C3), BF16),
+        V((2, NCH, NX, KD, TOK, 128), BF16),
+        V((2, NCH, NY, PADD, 128), BF16),
+        V((2, NCH, NZ, BLK, H1), BF16),
+        V((2, NCH, NX, NZ, TOK, H3), BF16),
+        V((2, NCH, NY, BLK, H3), BF16),
+        V((RING, NY, PADD, 128), BF16),
+        V((RING, NY, BLK, H3), BF16),
+        V((RING, 2, BLK, H1), BF16),
+        V((NCH, 2, HD, H1), BF16),
+        V((2, ROWS, HD), BF16),
+        V((2, 2, ROWS, HD), BF16),
         V((DEEP, NZ, BLK, C1), BF16),
         V((RING, 2, BLK, C1), BF16),
         V((2, NCH, BLK, C1), BF16),
@@ -544,6 +628,10 @@
         pltpu.SemaphoreType.DMA((8,)),
         pltpu.SemaphoreType.DMA((8,)),
         pltpu.SemaphoreType.DMA((RING,)),
+        pltpu.SemaphoreType.DMA((NCH, 2)),
+        pltpu.SemaphoreType.DMA((NCH, 2)),
+        pltpu.SemaphoreType.DMA((2,)),
+        pltpu.SemaphoreType.DMA((2, 2)),
     ]
     flops = 4 * 2 * ROWS * D * HD * 3
     return pl.pallas_call(

time: 265 us -> 251 us (0.947)
  Pallas kernels: 255 us -> 240 us
    pallas_call x1, Pallas kernels: 255 us -> 240 us  [layers(): pl.pallas_call(kernel, out_shape=jax.ShapeDtypeStruct((4, TOK, D), BF16),...]
where the time goes in v3:
time: 251 us; the launch traced here: 250 us
  Pallas kernels  240 us (96%)
  local copies, waits for them, and re-layouts  8.54 us (3%)
    pallas_call x1, Pallas kernels, layers(): pl.pallas_call(kernel, out_shape=jax.ShapeDtypeStruct((4, TOK, D), BF16),...  240 us

profile of v3, /device:TPU:0, one launch (start us, length us, event | category | flops | bytes accessed | tf_op | source)
XLA Modules:
  0.0 250.4 jit_solution(294337878317351821)
XLA Ops:
  0.6 0.8 copy.39
  1.4 0.1 copy.41
  1.5 0.2 convert_reduce_fusion
  1.7 0.1 copy.43
  1.9 0.1 copy.44
  2.0 0.7 maximum_bitcast_fusion
  2.7 0.7 tile.9.meta_ref
  3.4 4.1 %reshape_squeeze.4.saved_ref = bf16[4,640,256]{2,1,0:T(8,128)(2,1)} reshape(bf16[1,4,320,2,256]{4,3,2,1,0:T(2,128)(2,1)} %param.30) | data formatting | bytes 2621440 | tf_op jit(solution)/shard_map/reshape;squeeze | solution.py:667
  7.5 240.2 %relay_layers.1 = bf16[4,32,7168]{2,1,0:T(8,128)(2,1)} custom-call(bf16[32,7168]{1,0:T(8,128)(2,1)} %bitcast.20, bf16[32,7168]{1,0:T(8,128)(2,1)} %bitcast.21, bf16[32,7168]{1,0:T(8,128)(2,1)} %na_ref.1, bf16[32,7168]{1,0:T(8,128)(2,1)} %nb_ref.1, f32[32,128]{1,0:T(8,128)} %tile.9.meta_ref, bf16[4,640,256]{2,1,0:T(8,128)(2,1)} %reshape_squeeze.4.saved_ref, ...), custom_call_target="tpu_custom_call" | custom-call | flops 14092861440 | bytes 16777216 | tf_op jit(solution)/shard_map/relay_layers/pallas_call | solution.py:637
  247.7 2.7 %fusion.1 = (bf16[1,32,7168]{2,1,0:T(8,128)(2,1)}, bf16[1,32,7168]{2,1,0:T(8,128)(2,1)}, bf16[1,32,7168]{2,1,0:T(8,128)(2,1)}, bf16[1,32,7168]{2,1,0:T(8,128)(2,1)}) fusion(bf16[4,32,7168]{2,1,0:T(8,128)(2,1)} %relay_layers.1), kind=kLoop, calls=%fused_computation.5 | loop fusion | bytes 3670016 | tf_op jit(solution)/shard_map/slice | solution.py:671
  (3 shorter events, 0.1 us)

commit v4 on v3

--- a/solution.py
+++ b/solution.py
@@ -107,11 +107,11 @@
 
 
 def kernel(
-    xa_ref, xb_ref, na_ref, nb_ref, meta_ref, saved_ref, wg_ref, wu_ref, wdn_ref,
+    xa_ref, xb_ref, na_ref, nb_ref, ids_ref, probs_ref, saved_ref, wg_ref, wu_ref, wdn_ref,
     from3_ref, to3_ref, froms_ref, pick_ref, spread_ref,
     w3c_ref, w3r_ref, w1c_ref, w1r_ref, o3c_ref, o3r_ref, o1c_ref, o1r_ref, lane_ref,
     out_ref,
-    xin, ob, wgu, wd, svd, mr, mt, a1, a1t, pr1, a3, a3t, pr3, fg, fu, acc1, acc3, accp, gu1, gu3,
+    xin, ob, wgu, wd, svd, mr, mt, mb, a1, a1t, pr1, a3, a3t, pr3, fg, fu, acc1, acc3, accp, gu1, gu3,
     t1, y1, z1, t3, y3, y1s, y3s, zs, wp, hs, hr,
     q1, s1, r1a, r1b, y1rs, y1rr, tb1, x1r, q3, y3r, tb3, x3r, v3, s3, r3a, r3b,
     ss, rs, mss, mrs, ls, os, wss, wrs, hss, hrs,
@@ -165,6 +165,23 @@
     load(wg_ref, wgu.at[:, 0:HD], 6).start()
     load(wu_ref, wgu.at[:, HD:2 * HD], 7).start()
 
+    before = lax.broadcasted_iota(jnp.int32, (TOK, TOK), 0) < lax.broadcasted_iota(jnp.int32, (TOK, TOK), 1)
+    before = jnp.where(before, 1.0, 0.0).astype(BF16)
+    expert = lax.broadcasted_iota(jnp.int32, (EXPERTS, TOK), 0).astype(F32)
+    mb[...] = jnp.zeros_like(mb)
+    for m in range(4):
+        ids = ids_ref[m].astype(F32)
+        named = [expert == ids[k:k + 1] for k in range(TOPK)]
+        count = jnp.where(named[0], 1.0, 0.0) + jnp.where(named[1], 1.0, 0.0)
+        earlier = dot(count.astype(BF16), before)
+        for k in range(TOPK):
+            rank = jnp.sum(jnp.where(named[k], earlier, 0.0), axis=0, keepdims=True)
+            mb[m * 8 + k:m * 8 + k + 1, 0:TOK] = ids[k:k + 1] * float(CAP) + rank
+        mb[m * 8 + 2:m * 8 + 4, 0:TOK] = probs_ref[m]
+    tile = mb[...]
+    tile = tile + pltpu.roll(tile, TOK, 1)
+    mb[...] = tile + pltpu.roll(tile, 2 * TOK, 1)
+
     barrier = pltpu.get_barrier_semaphore()
     metas = [(dx, dz) for dx in range(NX) for dz in range(NZ) if dx or dz]
     for dx, dz in metas:
@@ -184,11 +201,11 @@
     pl.semaphore_wait(barrier, len(metas) + NY - 1 + in_pipe)
 
     src_me = x * NZ + z
-    mr[src_me] = meta_ref[...]
+    mr[src_me] = mb[...]
 
     def meta_copy(k, dx, dz, landing):
         return pltpu.make_async_remote_copy(
-            src_ref=meta_ref, dst_ref=mr.at[landing], send_sem=mss.at[k], recv_sem=mrs.at[k],
+            src_ref=mb, dst_ref=mr.at[landing], send_sem=mss.at[k], recv_sem=mrs.at[k],
             device_id=dev((x + dx) % NX, y, (z + dz) % NZ), device_id_type=MESH,
         )
 
@@ -254,7 +271,7 @@
         ).astype(BF16)
 
     def factors(st, m):
-        gu = dot(froms_ref[...], svd[m])
+        gu = dot(froms_ref[...], svd[m].reshape(2 * ROWS, HD))
         gate, up = gu[:ROWS], gu[ROWS:]
         sig = jax.nn.sigmoid(gate)
         fg[st] = up * sig * (1.0 + gate * (1.0 - sig))
@@ -308,14 +325,24 @@
         rcopy(mine, mine, Z3A + q, g, c, dev(x, y, d)).start()
         rcopy(xin.at[m, :, half_col(c, S1, 1 - half, H3)], mine, Z3A + 1 - q, g, c, dev(x, y, h)).start()
 
-        @pl.when((p == 0) & (st == 0))
-        def _():
-            @pl.when(g == 0)
+        @pl.when(g == 0)
+        def _():
+            load(wdn_ref, wd, 5).wait()
+
+        first = (4 * g + 2) // 3
+        for i in range(2):
+            now = first + i
+
+            @pl.when((now < 2 * NCH) & ((3 * now) // 4 == g))
             def _():
-                load(wdn_ref, wd, 5).wait()
-
-            weights(c, h, half, 0).start()
-            weights(c, h, half, 1).start()
+                _, _, other, side = pairing(now // 2)
+                cols = half_col(now // 2, (now % 2) * S1, 1 - side, H1)
+                pltpu.make_async_remote_copy(
+                    src_ref=wd.at[:, cols], dst_ref=wp.at[now // 2, now % 2],
+                    send_sem=wss.at[now // 2, now % 2], recv_sem=wrs.at[now // 2, now % 2],
+                    device_id=dev(x, y, other), device_id_type=MESH,
+                ).start()
+
 
         @pl.when(c == 1)
         def _():
@@ -569,7 +596,7 @@
     lax.fori_loop(0, UNITS + RETURN[-1], tick, 0)
 
 
-def layers(xa, xb, na, nb, meta, saved, wg, wu, wdn):
+def layers(xa, xb, na, nb, ids, probs, saved, wg, wu, wdn):
     consts = [jnp.asarray(a) for a in constants()]
     any_spec = pl.BlockSpec(memory_space=pl.ANY)
     vmem = pl.BlockSpec(memory_space=pltpu.VMEM)
@@ -579,9 +606,10 @@
         V((4, TOK, D), BF16),
         V((D, 2 * HD), BF16),
         V((HD, D), BF16),
-        V((4, 2 * ROWS, HD), BF16),
+        V((4, ROWS, 2, HD), BF16),
         V((NX * NZ, 32, 128), F32),
         V((NX * NZ, TOK, TOK), F32),
+        V((32, 128), F32),
         V((2, NY * PADD, NX * KD * TOK), BF16),
         V((2, NX * KG * TOK, NY * PADY), BF16),
         V((2, NY * PADD, 1), F32),
@@ -637,7 +665,7 @@
     return pl.pallas_call(
         kernel,
         out_shape=jax.ShapeDtypeStruct((4, TOK, D), BF16),
-        in_specs=[any_spec] * 4 + [vmem] + [any_spec] * 4 + [vmem] * len(consts),
+        in_specs=[any_spec] * 4 + [vmem] * 2 + [any_spec] * 4 + [vmem] * len(consts),
         out_specs=any_spec,
         scratch_shapes=scratch,
         compiler_params=pltpu.CompilerParams(
@@ -645,28 +673,16 @@
         ),
         cost_estimate=pl.CostEstimate(flops=flops, bytes_accessed=16 * 2**20, transcendentals=0),
         name="relay_layers",
-    )(xa, xb, na, nb, meta, saved, wg, wu, wdn, *consts)
-
-
-def route_data(ids, probs):
-    micro = ids.shape[0]
-    flat = ids.reshape(micro, TOK * TOPK)
-    pair = jnp.arange(TOK * TOPK)
-    earlier = (flat[:, :, None] == flat[:, None, :]) & (pair[None, :] < pair[:, None])
-    ranking = jnp.sum(earlier.astype(jnp.int32), axis=2)
-    slots = (flat * CAP + ranking).reshape(micro, TOK, TOPK).astype(F32)
-    both = jnp.concatenate([slots, probs], axis=2)
-    by_row = jnp.tile(both.transpose(0, 2, 1), (1, 2, 128 // TOK))
-    return by_row.reshape(micro * 8, 128)
+    )(xa, xb, na, nb, ids, probs, saved, wg, wu, wdn, *consts)
 
 
 def per_device(
     held_a, held_b, new_a, new_b, expert_ids, route_probs, saved_gate_up, w_gate, w_up, w_down
 ):
-    meta = route_data(expert_ids[0], route_probs[0])
-    saved = saved_gate_up[0].reshape(4, 2 * ROWS, HD)
+    ids, probs = expert_ids[0].transpose(0, 2, 1), route_probs[0].transpose(0, 2, 1)
+    saved = saved_gate_up[0]
     out = layers(
-        held_a[0], held_b[0], new_a, new_b, meta, saved, w_gate[0], w_up[0], w_down[0]
+        held_a[0], held_b[0], new_a, new_b, ids, probs, saved, w_gate[0], w_up[0], w_down[0]
     )
     return out[0][None], out[1][None], out[2][None], out[3][None]
 

time: 251 us -> 242 us (0.964)
  local copies, waits for them, and re-layouts: 8.54 us -> 2.69 us
    another operation x3 -> x0, local copies, waits for them, and re-layouts: 4.81 us -> none  [the longest x1 4.09 us: per_device(): saved = saved_gate_up[0].reshape(4, 2 * ROWS, HD)]
where the time goes in v4:
time: 242 us
  Pallas kernels  239 us (99%)
  local copies, waits for them, and re-layouts  2.69 us (1%)
    pallas_call x1, Pallas kernels, layers(): pl.pallas_call(kernel, out_shape=jax.ShapeDtypeStruct((4, TOK, D), BF16),...  239 us

profile of v4, /device:TPU:0, one launch (start us, length us, event | category | flops | bytes accessed | tf_op | source)
XLA Modules:
  0.0 241.9 jit_solution(5099959935755531428)
XLA Ops:
  0.6 238.5 %relay_layers.1 = bf16[4,32,7168]{2,1,0:T(8,128)(2,1)} custom-call(bf16[32,7168]{1,0:T(8,128)(2,1)} %bitcast.16, bf16[32,7168]{1,0:T(8,128)(2,1)} %bitcast.17, bf16[32,7168]{1,0:T(8,128)(2,1)} %na_ref.1, bf16[32,7168]{1,0:T(8,128)(2,1)} %nb_ref.1, s32[4,2,32]{2,1,0:T(2,128)} %bitcast.18, f32[4,2,32]{2,1,0:T(2,128)} %bitcast.19, ...), custom_call_target="tpu_custom_call" | custom-call | flops 14092861440 | bytes 16777216 | tf_op jit(solution)/shard_map/relay_layers/pallas_call | solution.py:665
  239.2 2.7 %fusion = (bf16[1,32,7168]{2,1,0:T(8,128)(2,1)}, bf16[1,32,7168]{2,1,0:T(8,128)(2,1)}, bf16[1,32,7168]{2,1,0:T(8,128)(2,1)}, bf16[1,32,7168]{2,1,0:T(8,128)(2,1)}) fusion(bf16[4,32,7168]{2,1,0:T(8,128)(2,1)} %relay_layers.1), kind=kLoop, calls=%fused_computation | loop fusion | bytes 3670016 | tf_op jit(solution)/shard_map/slice | solution.py:687
